TPU v7x, 32 devices: a whole 2x2x4 slice. The times are simulated.
32 devices in a mesh: member: 2 (over y), lon: 16 (over z, x, core).
Axes of the slice: x: 2, y: 2, z: 4, core: 2. Of those that a mesh axis runs over, the one named last changes fastest.
Arguments:
- state_start: float32 [190, 256, 128], P('member', 'lon'), parts along dimension 0, may hold values from -6 to 6
- lift_weight: bfloat16 [95, 256], replicated, may hold values from -0.625 to 0.625
- conv_kernel: float32 [49, 256], replicated, may hold values from -0.875 to 0.875
- norm_gain: float32 [256], replicated, may hold values from 0.1 to 1.9
- up_weight: bfloat16 [256, 1024], replicated, may hold values from -0.375 to 0.375
- down_weight: bfloat16 [1024, 256], replicated, may hold values from -0.1875 to 0.1875
- out_weight: bfloat16 [256, 95], replicated, may hold values from -0.375 to 0.375
- obs_cells: int32 [4, 256, 32, 4], P('member', 'lon'), parts along dimension 0, may hold values from 0 to 127
- obs_weights: float32 [4, 256, 32, 4], P('member', 'lon'), parts along dimension 0, may hold values from 0.1 to 1
- tile_counts: int32 [4, 256], P('member', 'lon'), parts along dimension 0, may hold values from 1 to 32, as said below
- obs_owner: int32 [4, 8192, 1], P('member', 'lon'), parts along dimension 0, may hold values from 0 to 15; in each aligned block of 512 rows (0 to 511, 512 to 1023, ..., all dimensions but the last counted through in order) at most 64 rows name the same one
- obs_values: float32 [4, 16, 16, 64, 95], P('member', 'lon'), parts along dimension 0, may hold values from -6 to 6
- obs_precision: float32 [4, 16, 16, 64, 95], P('member', 'lon'), parts along dimension 0, may hold values from 0.5 to 2
Outputs:
- gradient: float32 [190, 256, 128], P('member', 'lon'), parts along dimension 0
There are 2 independent parts, one for each index of `member`. A program takes and returns all parts, laid end to end along the dimension named above; an argument that names none is the same for every part. Nothing has to cross between parts.
Inputs may be any that keep to these rules, and one draw needn't show every extreme that they name: Slots k >= tile_counts of a tile are padding; some tile of every time holds 32 observations. `obs_owner`: within the 512 slots of one band at one time, no owner is named by more than 64 slots, and some band names one owner exactly 64 times.
All inputs are finite; a program needn't handle non-finite values.
Results may differ from a plain program's by a relative error of at most 0.015.
Values may be sent and summed in bfloat16 or wider, within the bound.
A program may use at most 128 MiB of HBM per device.

v0:
```python
import functools

import jax
import jax.numpy as jnp
from jax import lax
from jax.experimental import pallas as pl
from jax.experimental.pallas import tpu as pltpu
from jax.sharding import PartitionSpec as P

TILE_CELLS = 128


gelu_coef = 0.044715
root_two_pi = 0.7978845608028654
eps_norm = 1e-06
TAPS = 7
REACH = 3
VMEM_LIMIT = 56 * 1024 * 1024


def from_behind(value, axis, steps):
    count = lax.axis_size(axis)
    pairs = [(source, (source + steps) % count) for source in range(count)]
    return lax.ppermute(value, axis, pairs)


def edges(cells):
    west = from_behind(cells[-REACH:].astype(jnp.bfloat16), "lon", 1)
    east = from_behind(cells[:REACH].astype(jnp.bfloat16), "lon", -1)
    return west, east


def fill_padded(pad_ref, west_ref, mid_ref, east_ref):
    lon_rows, lat_cols, hidden = mid_ref.shape
    halves = hidden // 128
    zeros = jnp.zeros((8, 128), jnp.float32)

    def put(row, ref, at):
        for h in range(halves):
            pad_ref[h, row, 0:8, :] = zeros
            pad_ref[h, row, 8 + lat_cols : 16 + lat_cols, :] = zeros
            pad_ref[h, row, 8 : 8 + lat_cols, :] = ref[at, :, h * 128 : (h + 1) * 128].astype(
                jnp.float32
            )

    for row in range(REACH):
        put(row, west_ref, row)
        put(lon_rows + REACH + row, east_ref, row)

    def middle_row(row, carry):
        put(row + REACH, mid_ref, row)
        return carry

    lax.fori_loop(0, lon_rows, middle_row, 0)


def conv_block(pad_ref, kern_ref, mix_ref, lat_start):
    halves, lon_pad, _, _ = pad_ref.shape
    lon_rows = lon_pad - 2 * REACH

    def piece(step, carry):
        h, sub = step // 2, step % 2
        base = pl.multiple_of(lat_start + sub * 8, 8)
        sums = [None] * lon_rows
        for j in range(TAPS):
            weight = [kern_ref[h, i * TAPS + j] for i in range(TAPS)]
            for row in range(lon_pad):
                cells = pad_ref[h, row, pl.ds(base + j + 8 - REACH, 8), :]
                for i in range(TAPS):
                    o = row - i
                    if 0 <= o < lon_rows:
                        term = weight[i] * cells
                        sums[o] = term if sums[o] is None else sums[o] + term
        for o in range(lon_rows):
            mix_ref[h, o, pl.ds(pl.multiple_of(sub * 8, 8), 8), :] = sums[o]
        return carry

    lax.fori_loop(0, halves * 2, piece, 0)


def conv_norm_kernel(
    west_ref, mid_ref, east_ref, kern_ref, gain_ref, normal_ref, normed_ref, inverse_ref, pad_ref, mix_ref
):
    lon_rows, lat_cols, hidden = mid_ref.shape
    fill_padded(pad_ref, west_ref, mid_ref, east_ref)

    def block(at, carry):
        lat = pl.multiple_of(at * 16, 16)
        conv_block(pad_ref, kern_ref, mix_ref, lat)
        gain = gain_ref[...]
        for o in range(lon_rows):
            mixed = jnp.concatenate([mix_ref[h, o] for h in range(hidden // 128)], axis=1)
            center = mixed - jnp.mean(mixed, axis=1, keepdims=True)
            inverse = lax.rsqrt(jnp.mean(center * center, axis=1, keepdims=True) + eps_norm)
            normal = center * inverse
            normal_ref[o, pl.ds(lat, 16), :] = normal
            normed_ref[o, pl.ds(lat, 16), :] = (normal * gain).astype(jnp.bfloat16)
            inverse_ref[o, pl.ds(lat, 16), :] = jnp.broadcast_to(inverse, (16, 128))
        return carry

    lax.fori_loop(0, lat_cols // 16, block, 0)


def conv_add_kernel(west_ref, mid_ref, east_ref, kern_ref, add_ref, out_ref, pad_ref, mix_ref):
    lon_rows, lat_cols, hidden = mid_ref.shape
    fill_padded(pad_ref, west_ref, mid_ref, east_ref)

    def block(at, carry):
        lat = pl.multiple_of(at * 16, 16)
        conv_block(pad_ref, kern_ref, mix_ref, lat)
        for o in range(lon_rows):
            summed = jnp.concatenate([mix_ref[h, o] for h in range(hidden // 128)], axis=1)
            out_ref[o, pl.ds(lat, 16), :] = (add_ref[o, pl.ds(lat, 16), :] + summed).astype(
                jnp.bfloat16
            )
        return carry

    lax.fori_loop(0, lat_cols // 16, block, 0)


def conv_scratch(shape):
    lon_rows, lat_cols, hidden = shape
    halves = hidden // 128
    return [
        pltpu.VMEM((halves, lon_rows + 2 * REACH, lat_cols + 16, 128), jnp.float32),
        pltpu.VMEM((halves, lon_rows, 16, 128), jnp.float32),
    ]


def conv_cost(shape):
    cells = shape[0] * shape[1] * shape[2]
    return pl.CostEstimate(flops=cells * 98, bytes_accessed=cells * 12, transcendentals=0)


def in_vmem(count):
    return [pl.BlockSpec(memory_space=pltpu.VMEM)] * count


def conv_norm(cells, kern, gain):
    west, east = edges(cells)
    shape = cells.shape
    return pl.pallas_call(
        conv_norm_kernel,
        out_shape=(
            jax.ShapeDtypeStruct(shape, jnp.float32),
            jax.ShapeDtypeStruct(shape, jnp.bfloat16),
            jax.ShapeDtypeStruct(shape[:2] + (128,), jnp.float32),
        ),
        in_specs=in_vmem(5),
        out_specs=tuple(in_vmem(3)),
        scratch_shapes=conv_scratch(shape),
        cost_estimate=conv_cost(shape),
        compiler_params=pltpu.CompilerParams(vmem_limit_bytes=VMEM_LIMIT),
    )(west, cells, east, kern, gain)


def conv_add(cells, kern, add):
    west, east = edges(cells)
    shape = cells.shape
    return pl.pallas_call(
        conv_add_kernel,
        out_shape=jax.ShapeDtypeStruct(shape, jnp.bfloat16),
        in_specs=in_vmem(5),
        out_specs=pl.BlockSpec(memory_space=pltpu.VMEM),
        scratch_shapes=conv_scratch(shape),
        cost_estimate=conv_cost(shape),
        compiler_params=pltpu.CompilerParams(vmem_limit_bytes=VMEM_LIMIT),
    )(west, cells, east, kern, add)


def mlp_kernel(piece, normed_ref, lifted_ref, up_ref, down_ref, block_ref, slope_ref):
    normed = normed_ref[...]
    total = lifted_ref[...].astype(jnp.float32)
    for start in range(0, up_ref.shape[1], piece):
        z = jnp.dot(normed, up_ref[:, start : start + piece], preferred_element_type=jnp.float32)
        square = z * z
        tanh_val = jnp.tanh(z * (root_two_pi + root_two_pi * gelu_coef * square))
        half = 0.5 + 0.5 * tanh_val
        active = (z * half).astype(jnp.bfloat16)
        bend = z * (root_two_pi + 3.0 * root_two_pi * gelu_coef * square)
        slope = half + half * (1.0 - tanh_val) * bend
        slope_ref[:, start : start + piece] = slope.astype(jnp.bfloat16)
        total = total + jnp.dot(
            active, down_ref[start : start + piece, :], preferred_element_type=jnp.float32
        )
    block_ref[...] = total.astype(jnp.bfloat16)


def mlp(normed, lifted, up_weight, down_weight, rows=512, piece=256):
    amount, hidden = normed.shape
    wide = up_weight.shape[1]
    by_rows = lambda width: pl.BlockSpec((rows, width), lambda r: (r, 0))
    whole = lambda shape: pl.BlockSpec(shape, lambda r: (0, 0))
    return pl.pallas_call(
        functools.partial(mlp_kernel, piece),
        grid=(amount // rows,),
        out_shape=(
            jax.ShapeDtypeStruct((amount, hidden), jnp.bfloat16),
            jax.ShapeDtypeStruct((amount, wide), jnp.bfloat16),
        ),
        in_specs=[by_rows(hidden), by_rows(hidden), whole((hidden, wide)), whole((wide, hidden))],
        out_specs=(by_rows(hidden), by_rows(wide)),
        cost_estimate=pl.CostEstimate(
            flops=4 * amount * hidden * wide,
            bytes_accessed=amount * (wide + 3 * hidden) * 2,
            transcendentals=amount * wide,
        ),
        compiler_params=pltpu.CompilerParams(vmem_limit_bytes=VMEM_LIMIT),
    )(normed, lifted, up_weight, down_weight)


def mlp_back_kernel(
    piece, block_ref, slope_ref, normal_ref, inverse_ref, gain_ref, up_ref, down_ref, out_ref
):
    g_block = block_ref[...].astype(jnp.bfloat16)
    across = (((1,), (1,)), ((), ()))
    total = None
    for start in range(0, up_ref.shape[1], piece):
        g_active = lax.dot_general(
            g_block,
            down_ref[start : start + piece, :],
            across,
            preferred_element_type=jnp.float32,
        )
        g_middle = g_active * slope_ref[:, start : start + piece].astype(jnp.float32)
        term = lax.dot_general(
            g_middle.astype(jnp.bfloat16),
            up_ref[:, start : start + piece],
            across,
            preferred_element_type=jnp.float32,
        )
        total = term if total is None else total + term
    g_scaled = total * gain_ref[...]
    normal = normal_ref[...]
    out_ref[...] = inverse_ref[:, 0:1] * (
        g_scaled
        - jnp.mean(g_scaled, axis=1, keepdims=True)
        - normal * jnp.mean(g_scaled * normal, axis=1, keepdims=True)
    )


def mlp_back(g_block, slope, normal, inverse, gain, up_weight, down_weight, rows=512, piece=256):
    amount, hidden = g_block.shape
    wide = up_weight.shape[1]
    by_rows = lambda width: pl.BlockSpec((rows, width), lambda r: (r, 0))
    whole = lambda shape: pl.BlockSpec(shape, lambda r: (0, 0))
    return pl.pallas_call(
        functools.partial(mlp_back_kernel, piece),
        grid=(amount // rows,),
        out_shape=jax.ShapeDtypeStruct((amount, hidden), jnp.float32),
        in_specs=[
            by_rows(hidden),
            by_rows(wide),
            by_rows(hidden),
            by_rows(128),
            whole((1, hidden)),
            whole((hidden, wide)),
            whole((wide, hidden)),
        ],
        out_specs=by_rows(hidden),
        cost_estimate=pl.CostEstimate(
            flops=4 * amount * hidden * wide,
            bytes_accessed=amount * (2 * wide + 12 * hidden),
            transcendentals=0,
        ),
        compiler_params=pltpu.CompilerParams(vmem_limit_bytes=VMEM_LIMIT),
    )(g_block, slope, normal, inverse, gain, up_weight, down_weight)


def forward_step(state_field, weights):
    lift_weight, kern, _, gain, up_weight, down_weight, out_weight = weights
    channels, lon_rows, lat_cols = state_field.shape
    hidden = lift_weight.shape[1]
    lifted = lax.dot_general(
        state_field.astype(jnp.bfloat16),
        lift_weight,
        (((0,), (0,)), ((), ())),
        preferred_element_type=jnp.float32,
    ).astype(jnp.bfloat16)
    normal, normed, inverse = conv_norm(lifted, kern, gain)
    block_out, slope = mlp(
        normed.reshape(-1, hidden), lifted.reshape(-1, hidden), up_weight, down_weight
    )
    change = lax.dot_general(
        out_weight, block_out, (((0,), (1,)), ((), ())), preferred_element_type=jnp.float32
    )
    saved = (normal.reshape(-1, hidden), inverse.reshape(-1, 128), slope)
    return state_field + change.reshape(channels, lon_rows, lat_cols), saved


def backward_step(cotangent, saved, weights):
    lift_weight, _, flipped, gain, up_weight, down_weight, out_weight = weights
    normal, inverse, slope = saved
    channels, lon_rows, lat_cols = cotangent.shape
    hidden = lift_weight.shape[1]
    g_block = lax.dot_general(
        cotangent.astype(jnp.bfloat16),
        out_weight,
        (((0,), (1,)), ((), ())),
        preferred_element_type=jnp.float32,
    )
    g_mixed = mlp_back(
        g_block.reshape(-1, hidden), slope, normal, inverse, gain, up_weight, down_weight
    ).reshape(lon_rows, lat_cols, hidden)
    g_lifted = conv_add(g_mixed, flipped, g_block)
    g_state = lax.dot_general(
        lift_weight, g_lifted, (((1,), (2,)), ((), ())), preferred_element_type=jnp.float32
    )
    return cotangent + g_state


def tile_ops(cell_ids, point_weights):
    positions = jnp.arange(TILE_CELLS, dtype=jnp.int32)
    return jnp.sum(
        point_weights[..., None] * (cell_ids[..., None] == positions).astype(jnp.float32), axis=2
    )


def to_tiles(state_field):
    channels, lon_rows, lat_cols = state_field.shape
    tile_rows = TILE_CELLS // lon_rows
    split = state_field.reshape(channels, lon_rows, lat_cols // tile_rows, tile_rows)
    return split.transpose(2, 0, 1, 3).reshape(lat_cols // tile_rows, channels, TILE_CELLS)


def from_tiles(tile_sums, lon_rows):
    tile_total, channels, _ = tile_sums.shape
    tile_rows = TILE_CELLS // lon_rows
    split = tile_sums.reshape(tile_total, channels, lon_rows, tile_rows)
    return split.transpose(1, 2, 0, 3).reshape(channels, lon_rows, tile_total * tile_rows)


def slot_selector(owner_ids, band_count, place_count):
    hit = owner_ids[:, None] == jnp.arange(band_count, dtype=jnp.int32)[None, :]
    slots = jnp.arange(owner_ids.shape[0], dtype=jnp.int32)
    earlier = (slots[None, :] < slots[:, None]).astype(jnp.bfloat16)
    before = jnp.dot(earlier, hit.astype(jnp.bfloat16), preferred_element_type=jnp.float32)
    place = jnp.sum(jnp.where(hit, before, 0.0), axis=1).astype(jnp.int32)
    slot_code = owner_ids * place_count + place
    return (
        slot_code[:, None] == jnp.arange(band_count * place_count, dtype=jnp.int32)[None, :]
    ).astype(jnp.bfloat16)


def owners_data(obs_values, obs_precision):
    channels = obs_values.shape[-1]
    widen = ((0, 0), (0, 0), (0, 0), (0, 128 - channels))
    both = jnp.concatenate(
        [jnp.pad(part[:, 0].astype(jnp.bfloat16), widen) for part in (obs_values, obs_precision)],
        axis=3,
    ).transpose(1, 0, 2, 3)
    return lax.all_to_all(both, "lon", split_axis=0, concat_axis=0, tiled=True)


def shards(
    state_start,
    lift_weight,
    conv_kernel,
    norm_gain,
    up_weight,
    down_weight,
    out_weight,
    obs_cells,
    obs_weights,
    tile_counts,
    obs_owner,
    obs_values,
    obs_precision,
):
    hidden = norm_gain.shape[0]
    by_half = lambda taps: jnp.broadcast_to(
        taps.reshape(-1, 1, hidden // 128, 128).transpose(2, 0, 1, 3),
        (hidden // 128, taps.shape[0], 8, 128),
    )
    weights = (
        lift_weight,
        by_half(conv_kernel),
        by_half(conv_kernel[::-1]),
        norm_gain.reshape(1, hidden),
        up_weight,
        down_weight,
        out_weight,
    )
    channels, lon_rows = (state_start.shape[0], state_start.shape[1])
    band_count, place_count = (obs_values.shape[2], obs_values.shape[3])
    tile_total, slot_total = (obs_cells.shape[1], obs_cells.shape[2])
    arrived = owners_data(obs_values, obs_precision)
    operators = [
        tile_ops(obs_cells[moment], obs_weights[moment]).astype(jnp.bfloat16) for moment in range(2)
    ]
    state_one, saved_zero = forward_step(state_start, weights)
    state_two, saved_one = forward_step(state_one, weights)

    def pulled(moment, state_field):
        selector = slot_selector(obs_owner[moment, :, 0], band_count, place_count)
        chosen = jnp.dot(
            selector,
            arrived[:, moment].reshape(band_count * place_count, -1),
            preferred_element_type=jnp.float32,
        )
        live_slots = (
            (jnp.arange(slot_total, dtype=jnp.int32)[None, :] < tile_counts[moment][:, None])
            .astype(jnp.float32)
            .reshape(-1, 1)
        )
        model_equiv = jnp.einsum(
            "gkc,gsc->gks",
            operators[moment],
            to_tiles(state_field.astype(jnp.bfloat16)),
            preferred_element_type=jnp.float32,
        ).reshape(-1, channels)
        misfit = live_slots * (
            chosen[:, 128 : 128 + channels] * (model_equiv - chosen[:, :channels])
        )
        tile_sums = jnp.einsum(
            "gkc,gks->gsc",
            operators[moment],
            misfit.reshape(tile_total, slot_total, channels).astype(jnp.bfloat16),
            preferred_element_type=jnp.float32,
        )
        return from_tiles(tile_sums, lon_rows)

    carried = backward_step(pulled(1, state_two), saved_one, weights) + pulled(0, state_one)
    return backward_step(carried, saved_zero, weights)


def solution(mesh):
    placed = (
        P("member", "lon", None),
        P(),
        P(),
        P(),
        P(),
        P(),
        P(),
        P("member", "lon", None, None),
        P("member", "lon", None, None),
        P("member", "lon"),
        P("member", "lon", None),
        P("member", "lon", None, None, None),
        P("member", "lon", None, None, None),
    )
    return jax.shard_map(
        shards, mesh=mesh, in_specs=placed, out_specs=P("member", "lon", None), check_vma=False
    )
```

profile of v0, /device:TPU:0, one launch (start us, length us, event | category | flops | bytes accessed | tf_op | source)
XLA Modules:
  0.0 156.4 jit_solution(2614791912451292377)
XLA Ops:
  0.0 1.3 convert_element_type.121
  1.3 1.3 convolution_convert_fusion.1.mid_ref
  2.7 0.5 collective-permute-start
  3.2 5.0 %collective-permute-start.1 = (bf16[3,128,256]{2,1,0:T(8,128)(2,1)S(1)}, bf16[3,128,256]{2,1,0:T(8,128)(2,1)S(1)}, u32[]{:S(2)}, u32[]{:S(2)}) collective-permute-start(bf16[3,128,256]{2,1,0:T(8,128)(2,1)S(1)} %get-tuple-element.33), channel_id=1, source_target_pairs={{0,15},{1,0},{2,1},{3,2},{4,3},{5,4},{6,5},{7,6},{8,7},{9,8},{10,9... | collective-permute-start | bytes 589832 | tf_op jit(solution)/shard_map/ppermute | solution.py:24
  8.5 1.2 fusion.10
  9.8 4.3 %all-to-all-start = ((bf16[16,2,64,256]{3,2,1,0:T(8,128)(2,1)}), bf16[16,2,64,256]{3,2,1,0:T(8,128)(2,1)}, u32[]{:S(2)}, u32[]{:S(2)}) async-start(bf16[16,2,64,256]{3,2,1,0:T(8,128)(2,1)} %fusion.10), calls=%async_computation | async-start | bytes 2097152 | tf_op jit(solution)/shard_map/all_to_all | solution.py:352
  14.6 0.6 convert_add_fusion
  15.3 0.7 reshape.185
  16.2 0.6 convert_add_fusion.1
  16.8 0.7 reshape.184
  17.5 1.5 select_reduce_fusion
  19.0 0.8 broadcast_in_dim.15.kern_ref
  19.9 14.9 %shard_map.127 = (f32[16,128,256]{2,1,0:T(8,128)}, bf16[16,128,256]{2,1,0:T(8,128)(2,1)}, f32[16,128,128]{2,1,0:T(8,128)}) custom-call(bf16[3,128,256]{2,1,0:T(8,128)(2,1)} %copy-done.11, bf16[16,128,256]{2,1,0:T(8,128)(2,1)} %copy-done.2, bf16[3,128,256]{2,1,0:T(8,128)(2,1)} %copy-done.12, f32[2,49,8,128]{3,2,1,0:T(8,128)} %broadcast_in_dim.15.kern_ref, ...), custom_call_target="tpu_custom_call" | custom-call | flops 51380224 | bytes 6291456 | tf_op jit(solution)/shard_map/pallas_call | solution.py:142
  34.7 8.0 %shard_map.128 = (bf16[2048,256]{1,0:T(8,128)(2,1)}, bf16[2048,1024]{1,0:T(8,128)(2,1)}) custom-call(bf16[2048,256]{1,0:T(8,128)(2,1)} %bitcast.171, bf16[2048,256]{1,0:T(8,128)(2,1)} %bitcast.141, bf16[256,1024]{1,0:T(8,128)(2,1)} %up_ref.7, bf16[1024,256]{1,0:T(8,128)(2,1)} %down_ref.7), custom_call_target="tpu_custom_call" | custom-call | flops 2147483648 | bytes 7340032 | tf_op jit(solution)/shard_map/pallas_call | solution.py:194
  42.7 1.7 %fusion.54 = f32[2048,95]{0,1:T(8,128)S(1)} fusion(bf16[2048,256]{1,0:T(8,128)(2,1)} %get-tuple-element.16, bf16[256,95]{0,1:T(8,128)(2,1)S(1)} %copy-done), kind=kOutput, calls=%fused_computation.93 | convolution fusion | flops 99614720 | bytes 1875456 | tf_op jit(solution)/shard_map/dot_general | solution.py:284
  44.7 0.4 copy.129
  45.7 0.8 fusion.51
  46.7 4.2 %collective-permute-start.3 = (bf16[3,128,256]{2,1,0:T(8,128)(2,1)}, bf16[3,128,256]{2,1,0:T(8,128)(2,1)}, u32[]{:S(2)}, u32[]{:S(2)}) collective-permute-start(bf16[3,128,256]{2,1,0:T(8,128)(2,1)} %get-tuple-element.31), channel_id=1, source_target_pairs={{0,15},{1,0},{2,1},{3,2},{4,3},{5,4},{6,5},{7,6},{8,7},{9,8},{10,9... | collective-permute-start | bytes 589832 | tf_op jit(solution)/shard_map/ppermute | solution.py:24
  51.0 0.9 fusion.16
  51.9 1.1 copy.132
  53.0 1.7 %collective-permute-done.2.west_ref = bf16[3,128,256]{2,1,0:T(8,128)(2,1)} collective-permute-done((bf16[3,128,256]{2,1,0:T(8,128)(2,1)}, bf16[3,128,256]{2,1,0:T(8,128)(2,1)}, u32[]{:S(2)}, u32[]{:S(2)}) %collective-permute-start.2) | collective-permute-done | bytes 196640 | tf_op jit(solution)/shard_map/ppermute | solution.py:24
  54.7 14.8 %shard_map.129 = (f32[16,128,256]{2,1,0:T(8,128)}, bf16[16,128,256]{2,1,0:T(8,128)(2,1)}, f32[16,128,128]{2,1,0:T(8,128)}) custom-call(bf16[3,128,256]{2,1,0:T(8,128)(2,1)} %collective-permute-done.2.west_ref, bf16[16,128,256]{2,1,0:T(8,128)(2,1)} %copy-done.3, bf16[3,128,256]{2,1,0:T(8,128)(2,1)} %collective-permute-done.3.east_ref, ...), custom_call_target="tpu_custom_call" | custom-call | flops 51380224 | bytes 6291456 | tf_op jit(solution)/shard_map/pallas_call | solution.py:142
  69.5 8.0 %shard_map.130 = (bf16[2048,256]{1,0:T(8,128)(2,1)}, bf16[2048,1024]{1,0:T(8,128)(2,1)}) custom-call(bf16[2048,256]{1,0:T(8,128)(2,1)} %bitcast.170, bf16[2048,256]{1,0:T(8,128)(2,1)} %bitcast.142, bf16[256,1024]{1,0:T(8,128)(2,1)} %up_ref.7, bf16[1024,256]{1,0:T(8,128)(2,1)} %down_ref.7), custom_call_target="tpu_custom_call" | custom-call | flops 2147483648 | bytes 7340032 | tf_op jit(solution)/shard_map/pallas_call | solution.py:194
  77.5 1.7 %fusion.55 = f32[2048,95]{0,1:T(8,128)S(1)} fusion(bf16[2048,256]{1,0:T(8,128)(2,1)} %get-tuple-element.18, bf16[256,95]{0,1:T(8,128)(2,1)S(1)} %copy-done), kind=kOutput, calls=%fused_computation.94 | convolution fusion | flops 99614720 | bytes 1875456 | tf_op jit(solution)/shard_map/dot_general | solution.py:284
  79.6 0.4 copy.119
  80.4 1.3 fusion.50
  81.7 0.7 fusion
  83.0 1.7 %fusion.22.add_ref = f32[16,128,256]{2,1,0:T(8,128)} fusion(bf16[256,95]{0,1:T(8,128)(2,1)S(1)} %copy-done, f32[95,16,16,8]{0,3,1,2:T(8,128)S(1)} %convolution_bitcast_fusion.1), kind=kOutput, calls=%fused_computation.45 | convolution fusion | flops 99614720 | bytes 2924032 | tf_op jit(solution)/shard_map/dot_general | solution.py:296
  84.7 8.3 %shard_map.131 = f32[2048,256]{1,0:T(8,128)} custom-call(f32[2048,256]{1,0:T(8,128)} %bitcast.135, bf16[2048,1024]{1,0:T(8,128)(2,1)} %get-tuple-element.19.slope_ref, f32[2048,256]{1,0:T(8,128)} %bitcast.149, f32[2048,128]{1,0:T(8,128)} %bitcast.151, f32[1,256]{1,0:T(1,128)} %bitcast.164, bf16[256,1024]{1,0:T(8,128)(2,1)} %up_ref.7, bf16[1024,256]{1,0:T(8,128)(2,1)} %down_ref.7), custom_call_target="tpu_custom_call" | custom-call | flops 2147483648 | bytes 10485760 | tf_op jit(solution)/shard_map/pallas_call | solution.py:247
  93.0 1.7 %convert.10 = bf16[2048,256]{1,0:T(8,128)(2,1)S(1)} convert(f32[2048,256]{1,0:T(8,128)} %shard_map.131) | non-fusion elementwise | flops 524288 | bytes 3145728 | tf_op jit(solution)/shard_map/convert.5
  94.7 0.8 fusion.49
  95.4 1.2 collective-permute-start.4
  96.6 3.3 %collective-permute-start.5 = (bf16[3,128,256]{2,1,0:T(8,128)(2,1)}, bf16[3,128,256]{2,1,0:T(8,128)(2,1)}, u32[]{:S(2)}, u32[]{:S(2)}) collective-permute-start(bf16[3,128,256]{2,1,0:T(8,128)(2,1)} %bitcast.32), channel_id=1, source_target_pairs={{0,15},{1,0},{2,1},{3,2},{4,3},{5,4},{6,5},{7,6},{8,7},{9,8},{10,9... | collective-permute-start | bytes 589832 | tf_op jit(solution)/shard_map/ppermute | solution.py:24
  99.9 0.7 fusion.1
  102.1 1.5 collective-permute-done.4.west_ref
  103.5 0.8 broadcast_in_dim.17.kern_ref
  104.3 13.4 %shard_map.132 = bf16[16,128,256]{2,1,0:T(8,128)(2,1)} custom-call(bf16[3,128,256]{2,1,0:T(8,128)(2,1)} %copy-done.8, f32[16,128,256]{2,1,0:T(8,128)} %bitcast.136, bf16[3,128,256]{2,1,0:T(8,128)(2,1)} %collective-permute-done.5.east_ref, f32[2,49,8,128]{3,2,1,0:T(8,128)} %broadcast_in_dim.17.kern_ref, f32[16,128,256]{2,1,0:T(8,128)} %fusion.22.add_ref), custom_call_target="tpu_custom_call" | custom-call | flops 51380224 | bytes 6291456 | tf_op jit(solution)/shard_map/pallas_call | solution.py:160
  117.7 1.7 %fusion.5 = f32[95,16,128]{2,0,1:T(8,128)S(1)} fusion(f32[95,16,128]{2,0,1:T(8,128)S(1)} %copy.136, f32[95,16,128]{2,0,1:T(8,128)S(1)} %copy.128, bf16[16,128,256]{2,1,0:T(8,128)(2,1)} %shard_map.132, bf16[95,256]{1,0:T(8,128)(2,1)S(1)} %copy-done.6), kind=kOutput, calls=%fused_computation.15 | convolution fusion | flops 100003840 | bytes 3431936 | tf_op jit(solution)/shard_map/dot_general | solution.py:306
  119.4 1.8 %fusion.25.add_ref = f32[16,128,256]{2,1,0:T(8,128)} fusion(f32[95,16,128]{2,0,1:T(8,128)S(1)} %fusion.5, bf16[256,95]{0,1:T(8,128)(2,1)S(1)} %copy-done), kind=kOutput, calls=%fused_computation.48 | convolution fusion | flops 99809280 | bytes 2924032 | tf_op jit(solution)/shard_map/dot_general | solution.py:296
  121.3 8.3 %shard_map.133 = f32[2048,256]{1,0:T(8,128)} custom-call(f32[2048,256]{1,0:T(8,128)} %bitcast.137, bf16[2048,1024]{1,0:T(8,128)(2,1)} %get-tuple-element.22.slope_ref, f32[2048,256]{1,0:T(8,128)} %bitcast.148, f32[2048,128]{1,0:T(8,128)} %bitcast.150, f32[1,256]{1,0:T(1,128)} %bitcast.165, bf16[256,1024]{1,0:T(8,128)(2,1)} %up_ref.7, bf16[1024,256]{1,0:T(8,128)(2,1)} %down_ref.7), custom_call_target="tpu_custom_call" | custom-call | flops 2147483648 | bytes 10485760 | tf_op jit(solution)/shard_map/pallas_call | solution.py:247
  129.6 1.7 %convert.11 = bf16[2048,256]{1,0:T(8,128)(2,1)S(1)} convert(f32[2048,256]{1,0:T(8,128)} %shard_map.133) | non-fusion elementwise | flops 524288 | bytes 3145728 | tf_op jit(solution)/shard_map/convert.3
  131.3 0.6 collective-permute-start.6
  131.9 3.9 %collective-permute-start.7 = (bf16[3,128,256]{2,1,0:T(8,128)(2,1)S(1)}, bf16[3,128,256]{2,1,0:T(8,128)(2,1)S(1)}, u32[]{:S(2)}, u32[]{:S(2)}) collective-permute-start(bf16[3,128,256]{2,1,0:T(8,128)(2,1)S(1)} %bitcast.160), channel_id=1, source_target_pairs={{0,15},{1,0},{2,1},{3,2},{4,3},{5,4},{6,5},{7,6},{8,7},{9,8},{10,9... | collective-permute-start | bytes 589832 | tf_op jit(solution)/shard_map/ppermute | solution.py:24
  135.8 3.4 %collective-permute-done.6.west_ref = bf16[3,128,256]{2,1,0:T(8,128)(2,1)S(1)} collective-permute-done((bf16[3,128,256]{2,1,0:T(8,128)(2,1)S(1)}, bf16[3,128,256]{2,1,0:T(8,128)(2,1)S(1)}, u32[]{:S(2)}, u32[]{:S(2)}) %collective-permute-start.6) | collective-permute-done | bytes 196640 | tf_op jit(solution)/shard_map/ppermute | solution.py:24
  139.2 0.7 copy-done.9
  140.0 13.4 %shard_map.134 = bf16[16,128,256]{2,1,0:T(8,128)(2,1)} custom-call(bf16[3,128,256]{2,1,0:T(8,128)(2,1)} %copy-done.9, f32[16,128,256]{2,1,0:T(8,128)} %bitcast.138, bf16[3,128,256]{2,1,0:T(8,128)(2,1)} %copy-done.10, f32[2,49,8,128]{3,2,1,0:T(8,128)} %broadcast_in_dim.17.kern_ref, f32[16,128,256]{2,1,0:T(8,128)} %fusion.25.add_ref), custom_call_target="tpu_custom_call" | custom-call | flops 51380224 | bytes 6291456 | tf_op jit(solution)/shard_map/pallas_call | solution.py:160
  153.4 1.7 %fusion.6 = f32[95,16,128]{2,0,1:T(8,128)S(1)} fusion(f32[95,16,128]{2,0,1:T(8,128)S(1)} %fusion.5, bf16[16,128,256]{2,1,0:T(8,128)(2,1)} %shard_map.134, bf16[95,256]{1,0:T(8,128)(2,1)S(1)} %copy-done.6), kind=kOutput, calls=%fused_computation.16 | convolution fusion | flops 99809280 | bytes 2653696 | tf_op jit(solution)/shard_map/dot_general | solution.py:306
  155.1 1.3 copy.137
  (80 shorter events, 5.0 us)
Async XLA Ops:
  0.0 42.7 %copy-start = (bf16[256,95]{0,1:T(8,128)(2,1)S(1)}, bf16[256,95]{0,1:T(8,128)(2,1)}, u32[]{:S(2)}) copy-start(bf16[256,95]{0,1:T(8,128)(2,1)} %param.19) | copy-start | bytes 145924
  0.0 8.2 %copy-start.4 = (f32[2,1,16,64,95]{4,3,2,1,0:T(8,128)S(1)}, f32[2,1,16,64,95]{4,3,2,1,0:T(8,128)}, u32[]{:S(2)}) copy-start(f32[2,1,16,64,95]{4,3,2,1,0:T(8,128)} %param.24) | copy-start | bytes 2334724
  0.0 8.2 %copy-start.5 = (f32[2,1,16,64,95]{4,3,2,1,0:T(8,128)S(1)}, f32[2,1,16,64,95]{4,3,2,1,0:T(8,128)}, u32[]{:S(2)}) copy-start(f32[2,1,16,64,95]{4,3,2,1,0:T(8,128)} %param.25) | copy-start | bytes 2334724
  2.6 7.1 %copy-start.2 = (bf16[16,128,256]{2,1,0:T(8,128)(2,1)}, bf16[16,128,256]{2,1,0:T(8,128)(2,1)S(1)}, u32[]{:S(2)}) copy-start(bf16[16,128,256]{2,1,0:T(8,128)(2,1)S(1)} %convolution_convert_fusion.1.mid_ref) | copy-start | bytes 3145732
  2.7 16.3 %collective-permute-start = (bf16[3,128,256]{2,1,0:T(8,128)(2,1)S(1)}, bf16[3,128,256]{2,1,0:T(8,128)(2,1)S(1)}, u32[]{:S(2)}, u32[]{:S(2)}) collective-permute-start(bf16[3,128,256]{2,1,0:T(8,128)(2,1)S(1)} %get-tuple-element.34), channel_id=1, source_target_pairs={{0,1},{1,2},{2,3},{3,4},{4,5},{5,6},{6,7},{7,8},{8,9},{9,10},{10,1... | collective-permute-start | bytes 589832 | tf_op jit(solution)/shard_map/ppermute | solution.py:24
  3.2 15.8 %collective-permute-start.1 = (bf16[3,128,256]{2,1,0:T(8,128)(2,1)S(1)}, bf16[3,128,256]{2,1,0:T(8,128)(2,1)S(1)}, u32[]{:S(2)}, u32[]{:S(2)}) collective-permute-start(bf16[3,128,256]{2,1,0:T(8,128)(2,1)S(1)} %get-tuple-element.33), channel_id=1, source_target_pairs={{0,15},{1,0},{2,1},{3,2},{4,3},{5,4},{6,5},{7,6},{8,7},{9,8},{10,9... | collective-permute-start | bytes 589832 | tf_op jit(solution)/shard_map/ppermute | solution.py:24
  8.4 5.7 %copy-start.7 = (f32[49,256]{1,0:T(8,128)S(1)}, f32[49,256]{1,0:T(8,128)}, u32[]{:S(2)}) copy-start(f32[49,256]{1,0:T(8,128)} %param.15) | copy-start | bytes 150532
  8.5 5.8 %copy-start.13 = (f32[2,16,32,4]{2,3,1,0:T(4,128)S(1)}, f32[2,16,32,4]{2,3,1,0:T(4,128)}, u32[]{:S(2)}) copy-start(f32[2,16,32,4]{2,3,1,0:T(4,128)} %param.21) | copy-start | bytes 49156
  8.5 5.8 %copy-start.14 = (s32[2,16,32,4]{2,3,1,0:T(4,128)S(1)}, s32[2,16,32,4]{2,3,1,0:T(4,128)}, u32[]{:S(2)}) copy-start(s32[2,16,32,4]{2,3,1,0:T(4,128)} %param.20) | copy-start | bytes 49156
  8.5 5.8 %copy-start.17 = (s32[2,512,1]{1,2,0:T(1,128)S(1)}, s32[2,512,1]{1,2,0:T(1,128)}, u32[]{:S(2)}) copy-start(s32[2,512,1]{1,2,0:T(1,128)} %param.23) | copy-start | bytes 12292
  8.5 6.7 %copy-start.20 = (s32[2,16]{1,0:T(2,128)S(1)}, s32[2,16]{1,0:T(2,128)}, u32[]{:S(2)}) copy-start(s32[2,16]{1,0:T(2,128)} %param.22) | copy-start | bytes 388
  9.8 70.7 %all-to-all-start = ((bf16[16,2,64,256]{3,2,1,0:T(8,128)(2,1)}), bf16[16,2,64,256]{3,2,1,0:T(8,128)(2,1)}, u32[]{:S(2)}, u32[]{:S(2)}) async-start(bf16[16,2,64,256]{3,2,1,0:T(8,128)(2,1)} %fusion.10), calls=%async_computation | async-start | bytes 2097152 | tf_op jit(solution)/shard_map/all_to_all | solution.py:352
  19.0 0.9 copy-start.11
  19.0 0.9 copy-start.12
  42.7 1.9 %copy-start.1 = (f32[95,16,128]{2,1,0:T(8,128)S(1)}, f32[95,16,128]{2,1,0:T(8,128)}, u32[]{:S(2)}) copy-start(f32[95,16,128]{2,1,0:T(8,128)} %param.13) | copy-start | bytes 2334724
  44.4 0.8 copy-start.6
  45.7 9.1 %copy-start.3 = (bf16[16,128,256]{2,1,0:T(8,128)(2,1)}, bf16[16,128,256]{2,1,0:T(8,128)(2,1)S(1)}, u32[]{:S(2)}) copy-start(bf16[16,128,256]{2,1,0:T(8,128)(2,1)S(1)} %convolution_convert_fusion.mid_ref) | copy-start | bytes 3145732
  46.5 8.2 %collective-permute-start.2 = (bf16[3,128,256]{2,1,0:T(8,128)(2,1)}, bf16[3,128,256]{2,1,0:T(8,128)(2,1)}, u32[]{:S(2)}, u32[]{:S(2)}) collective-permute-start(bf16[3,128,256]{2,1,0:T(8,128)(2,1)} %get-tuple-element.32), channel_id=1, source_target_pairs={{0,1},{1,2},{2,3},{3,4},{4,5},{5,6},{6,7},{7,8},{8,9},{9,10},{10,1... | collective-permute-start | bytes 589832 | tf_op jit(solution)/shard_map/ppermute | solution.py:24
  46.7 8.0 %collective-permute-start.3 = (bf16[3,128,256]{2,1,0:T(8,128)(2,1)}, bf16[3,128,256]{2,1,0:T(8,128)(2,1)}, u32[]{:S(2)}, u32[]{:S(2)}) collective-permute-start(bf16[3,128,256]{2,1,0:T(8,128)(2,1)} %get-tuple-element.31), channel_id=1, source_target_pairs={{0,15},{1,0},{2,1},{3,2},{4,3},{5,4},{6,5},{7,6},{8,7},{9,8},{10,9... | collective-permute-start | bytes 589832 | tf_op jit(solution)/shard_map/ppermute | solution.py:24
  79.6 2.2 %copy-start.19 = (s32[512]{0:T(512)S(1)}, s32[512]{0:T(512)}, u32[]{:S(2)}) copy-start(s32[512]{0:T(512)} %convert_add_fusion.1) | copy-start | bytes 6148
  80.3 2.1 %copy-start.16 = (f32[512]{0:T(512)S(1)}, f32[512]{0:T(512)}, u32[]{:S(2)}) copy-start(f32[512]{0:T(512)} %reshape.184) | copy-start | bytes 6148
  93.0 6.9 %copy-start.18 = (s32[512]{0:T(512)S(1)}, s32[512]{0:T(512)}, u32[]{:S(2)}) copy-start(s32[512]{0:T(512)} %convert_add_fusion) | copy-start | bytes 6148
  93.0 7.6 %copy-start.15 = (f32[512]{0:T(512)S(1)}, f32[512]{0:T(512)}, u32[]{:S(2)}) copy-start(f32[512]{0:T(512)} %reshape.185) | copy-start | bytes 6148
  95.4 8.1 %collective-permute-start.4 = (bf16[3,128,256]{2,1,0:T(8,128)(2,1)}, bf16[3,128,256]{2,1,0:T(8,128)(2,1)S(1)}, u32[]{:S(2)}, u32[]{:S(2)}) collective-permute-start(bf16[3,128,256]{2,1,0:T(8,128)(2,1)} %bitcast.30), channel_id=1, source_target_pairs={{0,1},{1,2},{2,3},{3,4},{4,5},{5,6},{6,7},{7,8},{8,9},{9,10},{10,1... | collective-permute-start | bytes 589832 | tf_op jit(solution)/shard_map/ppermute | solution.py:24
  96.6 6.9 %collective-permute-start.5 = (bf16[3,128,256]{2,1,0:T(8,128)(2,1)}, bf16[3,128,256]{2,1,0:T(8,128)(2,1)}, u32[]{:S(2)}, u32[]{:S(2)}) collective-permute-start(bf16[3,128,256]{2,1,0:T(8,128)(2,1)} %bitcast.32), channel_id=1, source_target_pairs={{0,15},{1,0},{2,1},{3,2},{4,3},{5,4},{6,5},{7,6},{8,7},{9,8},{10,9... | collective-permute-start | bytes 589832 | tf_op jit(solution)/shard_map/ppermute | solution.py:24
  103.5 0.8 copy-start.8
  131.3 8.0 %collective-permute-start.6 = (bf16[3,128,256]{2,1,0:T(8,128)(2,1)S(1)}, bf16[3,128,256]{2,1,0:T(8,128)(2,1)S(1)}, u32[]{:S(2)}, u32[]{:S(2)}) collective-permute-start(bf16[3,128,256]{2,1,0:T(8,128)(2,1)S(1)} %bitcast.161), channel_id=1, source_target_pairs={{0,1},{1,2},{2,3},{3,4},{4,5},{5,6},{6,7},{7,8},{8,9},{9,10},{10,1... | collective-permute-start | bytes 589832 | tf_op jit(solution)/shard_map/ppermute | solution.py:24
  131.9 7.4 %collective-permute-start.7 = (bf16[3,128,256]{2,1,0:T(8,128)(2,1)S(1)}, bf16[3,128,256]{2,1,0:T(8,128)(2,1)S(1)}, u32[]{:S(2)}, u32[]{:S(2)}) collective-permute-start(bf16[3,128,256]{2,1,0:T(8,128)(2,1)S(1)} %bitcast.160), channel_id=1, source_target_pairs={{0,15},{1,0},{2,1},{3,2},{4,3},{5,4},{6,5},{7,6},{8,7},{9,8},{10,9... | collective-permute-start | bytes 589832 | tf_op jit(solution)/shard_map/ppermute | solution.py:24
  139.2 0.7 copy-start.9
  139.2 0.7 copy-start.10
where the time goes:
time: 157 us; the launch traced here: 156 us
  Pallas kernels  89 us (57%)
  starting transfers between devices  23.3 us (15%)
  matrix products  15.8 us (10%)
  local copies, waits for them, and re-layouts  12.2 us (8%)
  other arithmetic  9.09 us (6%)
  waiting for transfers between devices  6.63 us (4%)
    pallas_call x2, Pallas kernels, conv_norm(): pl.pallas_call(conv_norm_kernel, out_shape=(jax.ShapeDtypeStruct(shape, j...  29.7 us
    pallas_call x2, Pallas kernels, conv_add(): pl.pallas_call(conv_add_kernel, out_shape=jax.ShapeDtypeStruct(shape, jnp...  26.8 us
    ppermute x8, starting transfers between devices, from_behind(): return lax.ppermute(value, axis, pairs)  19 us
    pallas_call x2, Pallas kernels, mlp_back(): pl.pallas_call(functools.partial(mlp_back_kernel, piece), grid=(amount //...  16.6 us
    pallas_call x2, Pallas kernels, mlp(): pl.pallas_call(functools.partial(mlp_kernel, piece), grid=(amount // rows...  16 us
    ppermute x8, waiting for transfers between devices, from_behind(): return lax.ppermute(value, axis, pairs)  6.62 us
    all_to_all x1, starting transfers between devices, owners_data(): return lax.all_to_all(both, 'lon', split_axis=0, concat_axis=0, tiled=True)  4.34 us
    dot_general x2, matrix products, backward_step(): lax.dot_general(cotangent.astype(jnp.bfloat16), out_weight, (((0,), (1,))...  3.57 us
  transfers between devices with their start and end apart: 9, of which 3 were waited for; matrix products, arithmetic and copies ran while one was open for 11% of the time, Pallas kernels for 29%

commit v1 on v0

--- a/solution.py
+++ b/solution.py
@@ -18,104 +18,143 @@
 VMEM_LIMIT = 56 * 1024 * 1024
 
 
-def from_behind(value, axis, steps):
-    count = lax.axis_size(axis)
-    pairs = [(source, (source + steps) % count) for source in range(count)]
-    return lax.ppermute(value, axis, pairs)
-
-
-def edges(cells):
-    west = from_behind(cells[-REACH:].astype(jnp.bfloat16), "lon", 1)
-    east = from_behind(cells[:REACH].astype(jnp.bfloat16), "lon", -1)
-    return west, east
-
-
-def fill_padded(pad_ref, west_ref, mid_ref, east_ref):
-    lon_rows, lat_cols, hidden = mid_ref.shape
-    halves = hidden // 128
+def exchange(mid_ref, west_ref, east_ref, send_sem, recv_sem):
+    lon_rows = mid_ref.shape[0]
+    count = lax.axis_size("lon")
+    here = lax.axis_index("lon")
+    ahead, behind = lax.rem(here + 1, count), lax.rem(here + count - 1, count)
+    barrier = pltpu.get_barrier_semaphore()
+    for neighbour in (behind, ahead):
+        pl.semaphore_signal(
+            barrier,
+            inc=1,
+            device_id={"lon": neighbour},
+            device_id_type=pl.DeviceIdType.MESH,
+        )
+    pl.semaphore_wait(barrier, 2)
+    copies = []
+    for at, (source, target, neighbour) in enumerate(
+        (
+            (mid_ref.at[pl.ds(lon_rows - REACH, REACH)], west_ref, ahead),
+            (mid_ref.at[pl.ds(0, REACH)], east_ref, behind),
+        )
+    ):
+        copy = pltpu.make_async_remote_copy(
+            src_ref=source,
+            dst_ref=target,
+            send_sem=send_sem.at[at],
+            recv_sem=recv_sem.at[at],
+            device_id={"lon": neighbour},
+            device_id_type=pl.DeviceIdType.MESH,
+        )
+        copy.start()
+        copies.append(copy)
+    return copies
+
+
+def put_row(pad_ref, row, ref, at):
+    lat_cols, hidden = ref.shape[1:]
     zeros = jnp.zeros((8, 128), jnp.float32)
-
-    def put(row, ref, at):
-        for h in range(halves):
-            pad_ref[h, row, 0:8, :] = zeros
-            pad_ref[h, row, 8 + lat_cols : 16 + lat_cols, :] = zeros
-            pad_ref[h, row, 8 : 8 + lat_cols, :] = ref[at, :, h * 128 : (h + 1) * 128].astype(
-                jnp.float32
-            )
-
-    for row in range(REACH):
-        put(row, west_ref, row)
-        put(lon_rows + REACH + row, east_ref, row)
-
-    def middle_row(row, carry):
-        put(row + REACH, mid_ref, row)
-        return carry
-
-    lax.fori_loop(0, lon_rows, middle_row, 0)
-
-
-def conv_block(pad_ref, kern_ref, mix_ref, lat_start):
+    for h in range(hidden // 128):
+        pad_ref[h, row, 0:8, :] = zeros
+        pad_ref[h, row, 8 + lat_cols : 16 + lat_cols, :] = zeros
+        pad_ref[h, row, 8 : 8 + lat_cols, :] = ref[at, :, h * 128 : (h + 1) * 128].astype(
+            jnp.float32
+        )
+
+
+def conv_block(pad_ref, kern_ref, mix_ref, lat_start, wanted, flip):
     halves, lon_pad, _, _ = pad_ref.shape
-    lon_rows = lon_pad - 2 * REACH
+    last = TAPS * TAPS - 1
 
     def piece(step, carry):
         h, sub = step // 2, step % 2
         base = pl.multiple_of(lat_start + sub * 8, 8)
-        sums = [None] * lon_rows
+        sums = {}
         for j in range(TAPS):
-            weight = [kern_ref[h, i * TAPS + j] for i in range(TAPS)]
+            taps = [i * TAPS + j for i in range(TAPS)]
+            weight = [kern_ref[h, last - tap if flip else tap] for tap in taps]
             for row in range(lon_pad):
+                users = [(i, row - i) for i in range(TAPS) if row - i in wanted]
+                if not users:
+                    continue
                 cells = pad_ref[h, row, pl.ds(base + j + 8 - REACH, 8), :]
-                for i in range(TAPS):
-                    o = row - i
-                    if 0 <= o < lon_rows:
-                        term = weight[i] * cells
-                        sums[o] = term if sums[o] is None else sums[o] + term
-        for o in range(lon_rows):
+                for i, o in users:
+                    term = weight[i] * cells
+                    sums[o] = sums[o] + term if o in sums else term
+        for o in wanted:
             mix_ref[h, o, pl.ds(pl.multiple_of(sub * 8, 8), 8), :] = sums[o]
         return carry
 
     lax.fori_loop(0, halves * 2, piece, 0)
 
 
+def conv_all(mid_ref, kern_ref, pad_ref, mix_ref, west_ref, east_ref, sems, flip, finish):
+    lon_rows, lat_cols, _ = mid_ref.shape
+    copies = exchange(mid_ref, west_ref, east_ref, *sems)
+
+    def middle_row(row, carry):
+        put_row(pad_ref, row + REACH, mid_ref, row)
+        return carry
+
+    lax.fori_loop(0, lon_rows, middle_row, 0)
+    inner = tuple(range(REACH, lon_rows - REACH))
+    outer = tuple(o for o in range(lon_rows) if o not in inner)
+    blocks = lat_cols // 16
+
+    def run(first, end, wanted):
+        def block(at, carry):
+            lat = pl.multiple_of(at * 16, 16)
+            conv_block(pad_ref, kern_ref, mix_ref, lat, wanted, flip)
+            for o in wanted:
+                halves = [mix_ref[h, o] for h in range(mix_ref.shape[0])]
+                finish(o, lat, jnp.concatenate(halves, axis=1))
+            return carry
+
+        lax.fori_loop(first, end, block, 0)
+
+    run(0, blocks // 2, inner)
+    for copy in copies:
+        copy.wait()
+    for row in range(REACH):
+        put_row(pad_ref, row, west_ref, row)
+        put_row(pad_ref, lon_rows + REACH + row, east_ref, row)
+    run(0, blocks // 2, outer)
+    run(blocks // 2, blocks, tuple(range(lon_rows)))
+
+
 def conv_norm_kernel(
-    west_ref, mid_ref, east_ref, kern_ref, gain_ref, normal_ref, normed_ref, inverse_ref, pad_ref, mix_ref
+    mid_ref,
+    kern_ref,
+    gain_ref,
+    normal_ref,
+    normed_ref,
+    inverse_ref,
+    pad_ref,
+    mix_ref,
+    west_ref,
+    east_ref,
+    *sems,
 ):
-    lon_rows, lat_cols, hidden = mid_ref.shape
-    fill_padded(pad_ref, west_ref, mid_ref, east_ref)
-
-    def block(at, carry):
-        lat = pl.multiple_of(at * 16, 16)
-        conv_block(pad_ref, kern_ref, mix_ref, lat)
-        gain = gain_ref[...]
-        for o in range(lon_rows):
-            mixed = jnp.concatenate([mix_ref[h, o] for h in range(hidden // 128)], axis=1)
-            center = mixed - jnp.mean(mixed, axis=1, keepdims=True)
-            inverse = lax.rsqrt(jnp.mean(center * center, axis=1, keepdims=True) + eps_norm)
-            normal = center * inverse
-            normal_ref[o, pl.ds(lat, 16), :] = normal
-            normed_ref[o, pl.ds(lat, 16), :] = (normal * gain).astype(jnp.bfloat16)
-            inverse_ref[o, pl.ds(lat, 16), :] = jnp.broadcast_to(inverse, (16, 128))
-        return carry
-
-    lax.fori_loop(0, lat_cols // 16, block, 0)
-
-
-def conv_add_kernel(west_ref, mid_ref, east_ref, kern_ref, add_ref, out_ref, pad_ref, mix_ref):
-    lon_rows, lat_cols, hidden = mid_ref.shape
-    fill_padded(pad_ref, west_ref, mid_ref, east_ref)
-
-    def block(at, carry):
-        lat = pl.multiple_of(at * 16, 16)
-        conv_block(pad_ref, kern_ref, mix_ref, lat)
-        for o in range(lon_rows):
-            summed = jnp.concatenate([mix_ref[h, o] for h in range(hidden // 128)], axis=1)
-            out_ref[o, pl.ds(lat, 16), :] = (add_ref[o, pl.ds(lat, 16), :] + summed).astype(
-                jnp.bfloat16
-            )
-        return carry
-
-    lax.fori_loop(0, lat_cols // 16, block, 0)
+    def finish(o, lat, mixed):
+        center = mixed - jnp.mean(mixed, axis=1, keepdims=True)
+        inverse = lax.rsqrt(jnp.mean(center * center, axis=1, keepdims=True) + eps_norm)
+        normal = center * inverse
+        normal_ref[o, pl.ds(lat, 16), :] = normal.astype(jnp.bfloat16)
+        normed_ref[o, pl.ds(lat, 16), :] = (normal * gain_ref[...]).astype(jnp.bfloat16)
+        inverse_ref[o, pl.ds(lat, 16), :] = jnp.broadcast_to(inverse, (16, 128))
+
+    conv_all(mid_ref, kern_ref, pad_ref, mix_ref, west_ref, east_ref, sems, False, finish)
+
+
+def conv_add_kernel(
+    mid_ref, kern_ref, add_ref, out_ref, pad_ref, mix_ref, west_ref, east_ref, *sems
+):
+    def finish(o, lat, summed):
+        total = add_ref[o, pl.ds(lat, 16), :].astype(jnp.float32) + summed
+        out_ref[o, pl.ds(lat, 16), :] = total.astype(jnp.bfloat16)
+
+    conv_all(mid_ref, kern_ref, pad_ref, mix_ref, west_ref, east_ref, sems, True, finish)
 
 
 def conv_scratch(shape):
@@ -124,6 +163,10 @@
     return [
         pltpu.VMEM((halves, lon_rows + 2 * REACH, lat_cols + 16, 128), jnp.float32),
         pltpu.VMEM((halves, lon_rows, 16, 128), jnp.float32),
+        pltpu.VMEM((REACH, lat_cols, hidden), jnp.bfloat16),
+        pltpu.VMEM((REACH, lat_cols, hidden), jnp.bfloat16),
+        pltpu.SemaphoreType.DMA((2,)),
+        pltpu.SemaphoreType.DMA((2,)),
     ]
 
 
@@ -137,35 +180,37 @@
 
 
 def conv_norm(cells, kern, gain):
-    west, east = edges(cells)
     shape = cells.shape
     return pl.pallas_call(
         conv_norm_kernel,
         out_shape=(
-            jax.ShapeDtypeStruct(shape, jnp.float32),
+            jax.ShapeDtypeStruct(shape, jnp.bfloat16),
             jax.ShapeDtypeStruct(shape, jnp.bfloat16),
             jax.ShapeDtypeStruct(shape[:2] + (128,), jnp.float32),
         ),
-        in_specs=in_vmem(5),
+        in_specs=in_vmem(3),
         out_specs=tuple(in_vmem(3)),
         scratch_shapes=conv_scratch(shape),
         cost_estimate=conv_cost(shape),
-        compiler_params=pltpu.CompilerParams(vmem_limit_bytes=VMEM_LIMIT),
-    )(west, cells, east, kern, gain)
+        compiler_params=pltpu.CompilerParams(
+            vmem_limit_bytes=VMEM_LIMIT, collective_id=0, has_side_effects=True
+        ),
+    )(cells, kern, gain)
 
 
 def conv_add(cells, kern, add):
-    west, east = edges(cells)
     shape = cells.shape
     return pl.pallas_call(
         conv_add_kernel,
         out_shape=jax.ShapeDtypeStruct(shape, jnp.bfloat16),
-        in_specs=in_vmem(5),
+        in_specs=in_vmem(3),
         out_specs=pl.BlockSpec(memory_space=pltpu.VMEM),
         scratch_shapes=conv_scratch(shape),
         cost_estimate=conv_cost(shape),
-        compiler_params=pltpu.CompilerParams(vmem_limit_bytes=VMEM_LIMIT),
-    )(west, cells, east, kern, add)
+        compiler_params=pltpu.CompilerParams(
+            vmem_limit_bytes=VMEM_LIMIT, collective_id=1, has_side_effects=True
+        ),
+    )(cells, kern, add)
 
 
 def mlp_kernel(piece, normed_ref, lifted_ref, up_ref, down_ref, block_ref, slope_ref):
@@ -212,7 +257,7 @@
 def mlp_back_kernel(
     piece, block_ref, slope_ref, normal_ref, inverse_ref, gain_ref, up_ref, down_ref, out_ref
 ):
-    g_block = block_ref[...].astype(jnp.bfloat16)
+    g_block = block_ref[...]
     across = (((1,), (1,)), ((), ()))
     total = None
     for start in range(0, up_ref.shape[1], piece):
@@ -231,12 +276,13 @@
         )
         total = term if total is None else total + term
     g_scaled = total * gain_ref[...]
-    normal = normal_ref[...]
-    out_ref[...] = inverse_ref[:, 0:1] * (
+    normal = normal_ref[...].astype(jnp.float32)
+    g_mixed = inverse_ref[:, 0:1] * (
         g_scaled
         - jnp.mean(g_scaled, axis=1, keepdims=True)
         - normal * jnp.mean(g_scaled * normal, axis=1, keepdims=True)
     )
+    out_ref[...] = g_mixed.astype(jnp.bfloat16)
 
 
 def mlp_back(g_block, slope, normal, inverse, gain, up_weight, down_weight, rows=512, piece=256):
@@ -247,7 +293,7 @@
     return pl.pallas_call(
         functools.partial(mlp_back_kernel, piece),
         grid=(amount // rows,),
-        out_shape=jax.ShapeDtypeStruct((amount, hidden), jnp.float32),
+        out_shape=jax.ShapeDtypeStruct((amount, hidden), jnp.bfloat16),
         in_specs=[
             by_rows(hidden),
             by_rows(wide),
@@ -260,7 +306,7 @@
         out_specs=by_rows(hidden),
         cost_estimate=pl.CostEstimate(
             flops=4 * amount * hidden * wide,
-            bytes_accessed=amount * (2 * wide + 12 * hidden),
+            bytes_accessed=amount * (2 * wide + 8 * hidden),
             transcendentals=0,
         ),
         compiler_params=pltpu.CompilerParams(vmem_limit_bytes=VMEM_LIMIT),
@@ -268,7 +314,7 @@
 
 
 def forward_step(state_field, weights):
-    lift_weight, kern, _, gain, up_weight, down_weight, out_weight = weights
+    lift_weight, kern, gain, up_weight, down_weight, out_weight = weights
     channels, lon_rows, lat_cols = state_field.shape
     hidden = lift_weight.shape[1]
     lifted = lax.dot_general(
@@ -289,7 +335,7 @@
 
 
 def backward_step(cotangent, saved, weights):
-    lift_weight, _, flipped, gain, up_weight, down_weight, out_weight = weights
+    lift_weight, kern, gain, up_weight, down_weight, out_weight = weights
     normal, inverse, slope = saved
     channels, lon_rows, lat_cols = cotangent.shape
     hidden = lift_weight.shape[1]
@@ -298,11 +344,11 @@
         out_weight,
         (((0,), (1,)), ((), ())),
         preferred_element_type=jnp.float32,
-    )
+    ).astype(jnp.bfloat16)
     g_mixed = mlp_back(
         g_block.reshape(-1, hidden), slope, normal, inverse, gain, up_weight, down_weight
     ).reshape(lon_rows, lat_cols, hidden)
-    g_lifted = conv_add(g_mixed, flipped, g_block)
+    g_lifted = conv_add(g_mixed, kern, g_block)
     g_state = lax.dot_general(
         lift_weight, g_lifted, (((1,), (2,)), ((), ())), preferred_element_type=jnp.float32
     )
@@ -375,7 +421,6 @@
     weights = (
         lift_weight,
         by_half(conv_kernel),
-        by_half(conv_kernel[::-1]),
         norm_gain.reshape(1, hidden),
         up_weight,
         down_weight,

time: 157 us -> 158 us (level)
  Pallas kernels: 89 us -> 119 us
  starting transfers between devices: 23.3 us -> 7.49 us
  waiting for transfers between devices: 6.63 us -> 0.01 us
  other arithmetic: 9.09 us -> 4.72 us
  local copies, waits for them, and re-layouts: 12.2 us -> 9.69 us
    pallas_call x2, Pallas kernels: 29.7 us -> 52.5 us  [conv_norm(): pl.pallas_call(conv_norm_kernel, out_shape=(jax.ShapeDtypeStruct(shape, j...]
    ppermute x8 -> x0, starting transfers between devices: 19 us -> none  [from_behind(): return lax.ppermute(value, axis, pairs)]
    pallas_call x2, Pallas kernels: 26.8 us -> 35.3 us  [conv_add(): pl.pallas_call(conv_add_kernel, out_shape=jax.ShapeDtypeStruct(shape, jnp...]
    ppermute x8 -> x0, waiting for transfers between devices: 6.62 us -> none  [from_behind(): return lax.ppermute(value, axis, pairs)]
    another operation x2 -> x0, other arithmetic: 3.39 us -> none
    all_to_all x1, starting transfers between devices: 4.34 us -> 7.49 us  [owners_data(): return lax.all_to_all(both, 'lon', split_axis=0, concat_axis=0, tiled=True)]
    slice x4 -> x0, local copies, waits for them, and re-layouts: 1.65 us -> none  [edges(): east = from_behind(cells[:REACH].astype(jnp.bfloat16), 'lon', -1)]
  transfers between devices with their start and end apart: 9 -> 1, of which waited for: 3 -> 0; matrix products, arithmetic and copies ran while one was open for 11% -> 10% of each run, Pallas kernels for 29% -> 44%
where the time goes in v1:
time: 158 us; the launch traced here: 157 us
  Pallas kernels  119 us (75%)
  matrix products  15.4 us (10%)
  local copies, waits for them, and re-layouts  9.69 us (6%)
  starting transfers between devices  7.49 us (5%)
  other arithmetic  4.72 us (3%)
    pallas_call x2, Pallas kernels, conv_norm(): pl.pallas_call(conv_norm_kernel, out_shape=(jax.ShapeDtypeStruct(shape, j...  52.5 us
    pallas_call x2, Pallas kernels, conv_add(): pl.pallas_call(conv_add_kernel, out_shape=jax.ShapeDtypeStruct(shape, jnp...  35.3 us
    pallas_call x2, Pallas kernels, mlp(): pl.pallas_call(functools.partial(mlp_kernel, piece), grid=(amount // rows...  16 us
    pallas_call x2, Pallas kernels, mlp_back(): pl.pallas_call(functools.partial(mlp_back_kernel, piece), grid=(amount //...  15.5 us
    all_to_all x1, starting transfers between devices, owners_data(): return lax.all_to_all(both, 'lon', split_axis=0, concat_axis=0, tiled=True)  7.49 us
    dot_general x2, matrix products, forward_step(): lax.dot_general(out_weight, block_out, (((0,), (1,)), ((), ())), preferre...  3.34 us
    dot_general x2, matrix products, backward_step(): lax.dot_general(lift_weight, g_lifted, (((1,), (2,)), ((), ())), preferre...  3.26 us
  transfers between devices with their start and end apart: 1, of which 0 were waited for; matrix products, arithmetic and copies ran while one was open for 10% of the time, Pallas kernels for 44%

profile of v1, /device:TPU:0, one launch (start us, length us, event | category | flops | bytes accessed | tf_op | source)
XLA Modules:
  0.0 156.8 jit_solution(10051662108774152307)
XLA Ops:
  0.0 1.8 %fusion.14 = (bf16[2,16,64,95]{3,2,0,1:T(8,128)(2,1)S(1)}, bf16[2,16,64,95]{3,2,0,1:T(8,128)(2,1)S(1)}) fusion(f32[2,1,16,64,95]{4,3,2,1,0:T(8,128)} %param.24, f32[2,1,16,64,95]{4,3,2,1,0:T(8,128)} %param.25), kind=kLoop, calls=%fused_computation.39 | loop fusion | bytes 2334720 | tf_op jit(solution)/shard_map/convert_element_type | solution.py:395
  1.8 1.3 fusion.10
  3.0 7.5 %all-to-all-start = ((bf16[16,2,64,256]{3,2,1,0:T(8,128)(2,1)}), bf16[16,2,64,256]{3,2,1,0:T(8,128)(2,1)S(1)}, u32[]{:S(2)}, u32[]{:S(2)}) async-start(bf16[16,2,64,256]{3,2,1,0:T(8,128)(2,1)} %fusion.10), calls=%async_computation | async-start | bytes 2097152 | tf_op jit(solution)/shard_map/all_to_all | solution.py:398
  10.7 1.4 convolution_convert_fusion.3.mid_ref
  12.1 0.8 broadcast_in_dim.11.kern_ref
  12.9 33.0 %shard_map.127 = (bf16[16,128,256]{2,1,0:T(8,128)(2,1)}, bf16[16,128,256]{2,1,0:T(8,128)(2,1)}, f32[16,128,128]{2,1,0:T(8,128)}) custom-call(bf16[16,128,256]{2,1,0:T(8,128)(2,1)} %convolution_convert_fusion.3.mid_ref, f32[2,49,8,128]{3,2,1,0:T(8,128)} %broadcast_in_dim.11.kern_ref, f32[1,256]{1,0:T(1,128)} %bitcast.150), custom_call_target="tpu_custom_call" | custom-call | flops 51380224 | bytes 6291456 | tf_op jit(solution)/shard_map/pallas_call | solution.py:184
  45.9 8.0 %shard_map.128 = (bf16[2048,256]{1,0:T(8,128)(2,1)}, bf16[2048,1024]{1,0:T(8,128)(2,1)}) custom-call(bf16[2048,256]{1,0:T(8,128)(2,1)} %bitcast.158, bf16[2048,256]{1,0:T(8,128)(2,1)} %bitcast.134, bf16[256,1024]{1,0:T(8,128)(2,1)} %up_ref.7, bf16[1024,256]{1,0:T(8,128)(2,1)} %down_ref.7), custom_call_target="tpu_custom_call" | custom-call | flops 2147483648 | bytes 7340032 | tf_op jit(solution)/shard_map/pallas_call | solution.py:239
  53.9 1.7 %fusion.48 = f32[2048,95]{0,1:T(8,128)S(1)} fusion(bf16[2048,256]{1,0:T(8,128)(2,1)} %get-tuple-element.16, bf16[256,95]{0,1:T(8,128)(2,1)S(1)} %copy-done), kind=kOutput, calls=%fused_computation.88 | convolution fusion | flops 99614720 | bytes 1875456 | tf_op jit(solution)/shard_map/dot_general | solution.py:330
  55.6 0.1 copy.138
  55.7 0.8 fusion.25
  56.6 1.4 copy.124
  58.0 1.4 convolution_convert_fusion.2.mid_ref
  59.4 19.5 %shard_map.129 = (bf16[16,128,256]{2,1,0:T(8,128)(2,1)}, bf16[16,128,256]{2,1,0:T(8,128)(2,1)}, f32[16,128,128]{2,1,0:T(8,128)}) custom-call(bf16[16,128,256]{2,1,0:T(8,128)(2,1)} %convolution_convert_fusion.2.mid_ref, f32[2,49,8,128]{3,2,1,0:T(8,128)} %broadcast_in_dim.11.kern_ref, f32[1,256]{1,0:T(1,128)} %bitcast.151), custom_call_target="tpu_custom_call" | custom-call | flops 51380224 | bytes 6291456 | tf_op jit(solution)/shard_map/pallas_call | solution.py:184
  78.8 8.0 %shard_map.130 = (bf16[2048,256]{1,0:T(8,128)(2,1)}, bf16[2048,1024]{1,0:T(8,128)(2,1)}) custom-call(bf16[2048,256]{1,0:T(8,128)(2,1)} %bitcast.159, bf16[2048,256]{1,0:T(8,128)(2,1)} %bitcast.135, bf16[256,1024]{1,0:T(8,128)(2,1)} %up_ref.7, bf16[1024,256]{1,0:T(8,128)(2,1)} %down_ref.7), custom_call_target="tpu_custom_call" | custom-call | flops 2147483648 | bytes 7340032 | tf_op jit(solution)/shard_map/pallas_call | solution.py:239
  86.8 1.7 %fusion.49 = f32[2048,95]{0,1:T(8,128)S(1)} fusion(bf16[2048,256]{1,0:T(8,128)(2,1)} %get-tuple-element.18, bf16[256,95]{0,1:T(8,128)(2,1)S(1)} %copy-done), kind=kOutput, calls=%fused_computation.89 | convolution fusion | flops 99614720 | bytes 1875456 | tf_op jit(solution)/shard_map/dot_general | solution.py:330
  88.5 0.1 copy.139
  88.7 0.9 fusion.13
  89.6 1.4 copy.115
  91.1 1.4 select_reduce_fusion
  92.5 0.2 fusion.18
  92.8 0.2 copy.118
  92.9 0.1 fusion.44
  93.0 0.1 reshape.172
  93.1 0.2 fusion.16
  93.3 0.2 copy.127
  93.5 0.1 reshape.173
  93.6 0.3 fusion.7
  93.9 0.3 fusion.8
  94.2 0.1 fusion.46
  94.2 0.7 fusion
  95.0 0.1 copy.119
  95.1 0.3 convolution_bitcast_fusion.1
  95.5 1.4 convolution_convert_fusion.1.add_ref
  96.9 0.1 copy.163
  97.0 7.8 %shard_map.131 = bf16[2048,256]{1,0:T(8,128)(2,1)} custom-call(bf16[2048,256]{1,0:T(8,128)(2,1)} %bitcast.127, bf16[2048,1024]{1,0:T(8,128)(2,1)} %get-tuple-element.19.slope_ref, bf16[2048,256]{1,0:T(8,128)(2,1)} %bitcast.141, f32[2048,128]{1,0:T(8,128)} %bitcast.142, f32[1,256]{1,0:T(1,128)} %bitcast.152, bf16[256,1024]{1,0:T(8,128)(2,1)} %up_ref.7, ...), custom_call_target="tpu_custom_call" | custom-call | flops 2147483648 | bytes 8388608 | tf_op jit(solution)/shard_map/pallas_call | solution.py:293
  104.7 17.8 %shard_map.132 = bf16[16,128,256]{2,1,0:T(8,128)(2,1)} custom-call(bf16[16,128,256]{2,1,0:T(8,128)(2,1)} %bitcast.131, f32[2,49,8,128]{3,2,1,0:T(8,128)} %broadcast_in_dim.11.kern_ref, bf16[16,128,256]{2,1,0:T(8,128)(2,1)} %convolution_convert_fusion.1.add_ref), custom_call_target="tpu_custom_call" | custom-call | flops 51380224 | bytes 6291456 | tf_op jit(solution)/shard_map/pallas_call | solution.py:203
  122.5 0.4 copy.123
  122.9 0.7 fusion.1
  123.6 0.1 copy.128
  123.8 0.4 convolution_bitcast_fusion
  124.1 0.1 copy.162
  124.2 1.3 copy.131
  125.5 1.6 %fusion.5 = f32[95,16,128]{2,0,1:T(8,128)S(1)} fusion(f32[95,16,128]{2,0,1:T(8,128)} %copy.131, f32[95,16,128]{2,0,1:T(8,128)S(1)} %copy.123, bf16[16,128,256]{2,1,0:T(8,128)(2,1)S(1)} %copy-done.2, bf16[95,256]{1,0:T(8,128)(2,1)S(1)} %copy-done.3), kind=kOutput, calls=%fused_computation.17 | convolution fusion | flops 100003840 | bytes 3431936 | tf_op jit(solution)/shard_map/dot_general | solution.py:352
  127.1 1.4 convolution_convert_fusion.add_ref
  128.5 7.7 %shard_map.133 = bf16[2048,256]{1,0:T(8,128)(2,1)} custom-call(bf16[2048,256]{1,0:T(8,128)(2,1)} %bitcast.126, bf16[2048,1024]{1,0:T(8,128)(2,1)} %get-tuple-element.22.slope_ref, bf16[2048,256]{1,0:T(8,128)(2,1)} %bitcast.139, f32[2048,128]{1,0:T(8,128)} %bitcast.140, f32[1,256]{1,0:T(1,128)} %bitcast.153, bf16[256,1024]{1,0:T(8,128)(2,1)} %up_ref.7, ...), custom_call_target="tpu_custom_call" | custom-call | flops 2147483648 | bytes 8388608 | tf_op jit(solution)/shard_map/pallas_call | solution.py:293
  136.3 17.6 %shard_map.134 = bf16[16,128,256]{2,1,0:T(8,128)(2,1)} custom-call(bf16[16,128,256]{2,1,0:T(8,128)(2,1)} %bitcast.130, f32[2,49,8,128]{3,2,1,0:T(8,128)} %broadcast_in_dim.11.kern_ref, bf16[16,128,256]{2,1,0:T(8,128)(2,1)} %convolution_convert_fusion.add_ref), custom_call_target="tpu_custom_call" | custom-call | flops 51380224 | bytes 6291456 | tf_op jit(solution)/shard_map/pallas_call | solution.py:203
  153.8 1.7 %fusion.6 = f32[95,16,128]{2,0,1:T(8,128)S(1)} fusion(f32[95,16,128]{2,0,1:T(8,128)S(1)} %fusion.5, bf16[16,128,256]{2,1,0:T(8,128)(2,1)} %shard_map.134, bf16[95,256]{1,0:T(8,128)(2,1)S(1)} %copy-done.3), kind=kOutput, calls=%fused_computation.18 | convolution fusion | flops 99809280 | bytes 2653696 | tf_op jit(solution)/shard_map/dot_general | solution.py:352
  155.5 1.3 copy.132
  (30 shorter events, 0.3 us)
Async XLA Ops:
  0.0 53.9 %copy-start = (bf16[256,95]{0,1:T(8,128)(2,1)S(1)}, bf16[256,95]{0,1:T(8,128)(2,1)}, u32[]{:S(2)}) copy-start(bf16[256,95]{0,1:T(8,128)(2,1)} %param.19) | copy-start | bytes 145924
  1.8 8.8 %copy-start.6 = (f32[49,256]{1,0:T(8,128)S(1)}, f32[49,256]{1,0:T(8,128)}, u32[]{:S(2)}) copy-start(f32[49,256]{1,0:T(8,128)} %param.15) | copy-start | bytes 150532
  1.8 8.8 %copy-start.1 = (f32[95,16,128]{2,1,0:T(8,128)S(1)}, f32[95,16,128]{2,1,0:T(8,128)}, u32[]{:S(2)}) copy-start(f32[95,16,128]{2,1,0:T(8,128)} %param.13) | copy-start | bytes 2334724
  3.0 7.6 %copy-start.3 = (bf16[95,256]{1,0:T(8,128)(2,1)S(1)}, bf16[95,256]{1,0:T(8,128)(2,1)}, u32[]{:S(2)}) copy-start(bf16[95,256]{1,0:T(8,128)(2,1)} %param.14) | copy-start | bytes 145924
  3.0 91.1 %all-to-all-start = ((bf16[16,2,64,256]{3,2,1,0:T(8,128)(2,1)}), bf16[16,2,64,256]{3,2,1,0:T(8,128)(2,1)S(1)}, u32[]{:S(2)}, u32[]{:S(2)}) async-start(bf16[16,2,64,256]{3,2,1,0:T(8,128)(2,1)} %fusion.10), calls=%async_computation | async-start | bytes 2097152 | tf_op jit(solution)/shard_map/all_to_all | solution.py:398
  88.6 2.4 %copy-start.4 = (s32[2,16,32,4]{2,3,1,0:T(4,128)S(1)}, s32[2,16,32,4]{2,3,1,0:T(4,128)}, u32[]{:S(2)}) copy-start(s32[2,16,32,4]{2,3,1,0:T(4,128)} %param.20) | copy-start | bytes 49156
  88.6 2.4 %copy-start.5 = (f32[2,16,32,4]{2,3,1,0:T(4,128)S(1)}, f32[2,16,32,4]{2,3,1,0:T(4,128)}, u32[]{:S(2)}) copy-start(f32[2,16,32,4]{2,3,1,0:T(4,128)} %param.21) | copy-start | bytes 49156
  89.6 3.3 %copy-start.8 = (s32[2,16]{1,0:T(2,128)S(1)}, s32[2,16]{1,0:T(2,128)}, u32[]{:S(2)}) copy-start(s32[2,16]{1,0:T(2,128)} %param.22) | copy-start | bytes 388
  89.6 4.0 %copy-start.7 = (s32[2,512,1]{1,2,0:T(1,128)S(1)}, s32[2,512,1]{1,2,0:T(1,128)}, u32[]{:S(2)}) copy-start(s32[2,512,1]{1,2,0:T(1,128)} %param.23) | copy-start | bytes 12292
  124.1 1.4 copy-start.2

commit v2 on v1

--- a/solution.py
+++ b/solution.py
@@ -16,6 +16,13 @@
 TAPS = 7
 REACH = 3
 VMEM_LIMIT = 56 * 1024 * 1024
+
+
+def edges(cells):
+    count = lax.axis_size("lon")
+    west = lax.ppermute(cells[-REACH:], "lon", [(i, (i + 1) % count) for i in range(count)])
+    east = lax.ppermute(cells[:REACH], "lon", [((i + 1) % count, i) for i in range(count)])
+    return west, east
 
 
 def exchange(mid_ref, west_ref, east_ref, send_sem, recv_sem):
@@ -91,7 +98,8 @@
 
 def conv_all(mid_ref, kern_ref, pad_ref, mix_ref, west_ref, east_ref, sems, flip, finish):
     lon_rows, lat_cols, _ = mid_ref.shape
-    copies = exchange(mid_ref, west_ref, east_ref, *sems)
+    copies = exchange(mid_ref, west_ref, east_ref, *sems) if sems else []
+    early = lat_cols // 64 if sems else 0
 
     def middle_row(row, carry):
         put_row(pad_ref, row + REACH, mid_ref, row)
@@ -113,14 +121,16 @@
 
         lax.fori_loop(first, end, block, 0)
 
-    run(0, blocks // 2, inner)
+    if early:
+        run(0, early, inner)
     for copy in copies:
         copy.wait()
     for row in range(REACH):
         put_row(pad_ref, row, west_ref, row)
         put_row(pad_ref, lon_rows + REACH + row, east_ref, row)
-    run(0, blocks // 2, outer)
-    run(blocks // 2, blocks, tuple(range(lon_rows)))
+    if early:
+        run(0, early, outer)
+    run(early, blocks, tuple(range(lon_rows)))
 
 
 def conv_norm_kernel(
@@ -147,6 +157,10 @@
     conv_all(mid_ref, kern_ref, pad_ref, mix_ref, west_ref, east_ref, sems, False, finish)
 
 
+def conv_norm_given_kernel(west_ref, east_ref, *refs):
+    conv_norm_kernel(*refs, west_ref, east_ref)
+
+
 def conv_add_kernel(
     mid_ref, kern_ref, add_ref, out_ref, pad_ref, mix_ref, west_ref, east_ref, *sems
 ):
@@ -179,23 +193,25 @@
     return [pl.BlockSpec(memory_space=pltpu.VMEM)] * count
 
 
-def conv_norm(cells, kern, gain):
+def conv_norm(cells, kern, gain, given):
     shape = cells.shape
     return pl.pallas_call(
-        conv_norm_kernel,
+        conv_norm_given_kernel if given else conv_norm_kernel,
         out_shape=(
             jax.ShapeDtypeStruct(shape, jnp.bfloat16),
             jax.ShapeDtypeStruct(shape, jnp.bfloat16),
             jax.ShapeDtypeStruct(shape[:2] + (128,), jnp.float32),
         ),
-        in_specs=in_vmem(3),
+        in_specs=in_vmem(5 if given else 3),
         out_specs=tuple(in_vmem(3)),
-        scratch_shapes=conv_scratch(shape),
+        scratch_shapes=conv_scratch(shape)[: 2 if given else None],
         cost_estimate=conv_cost(shape),
-        compiler_params=pltpu.CompilerParams(
+        compiler_params=pltpu.CompilerParams(vmem_limit_bytes=VMEM_LIMIT)
+        if given
+        else pltpu.CompilerParams(
             vmem_limit_bytes=VMEM_LIMIT, collective_id=0, has_side_effects=True
         ),
-    )(cells, kern, gain)
+    )(*(edges(cells) if given else ()), cells, kern, gain)
 
 
 def conv_add(cells, kern, add):
@@ -313,7 +329,7 @@
     )(g_block, slope, normal, inverse, gain, up_weight, down_weight)
 
 
-def forward_step(state_field, weights):
+def forward_step(state_field, weights, given):
     lift_weight, kern, gain, up_weight, down_weight, out_weight = weights
     channels, lon_rows, lat_cols = state_field.shape
     hidden = lift_weight.shape[1]
@@ -323,7 +339,7 @@
         (((0,), (0,)), ((), ())),
         preferred_element_type=jnp.float32,
     ).astype(jnp.bfloat16)
-    normal, normed, inverse = conv_norm(lifted, kern, gain)
+    normal, normed, inverse = conv_norm(lifted, kern, gain, given)
     block_out, slope = mlp(
         normed.reshape(-1, hidden), lifted.reshape(-1, hidden), up_weight, down_weight
     )
@@ -433,8 +449,8 @@
     operators = [
         tile_ops(obs_cells[moment], obs_weights[moment]).astype(jnp.bfloat16) for moment in range(2)
     ]
-    state_one, saved_zero = forward_step(state_start, weights)
-    state_two, saved_one = forward_step(state_one, weights)
+    state_one, saved_zero = forward_step(state_start, weights, True)
+    state_two, saved_one = forward_step(state_one, weights, False)
 
     def pulled(moment, state_field):
         selector = slot_selector(obs_owner[moment, :, 0], band_count, place_count)

time: 158 us -> 145 us (0.918)
  Pallas kernels: 119 us -> 105 us
  starting transfers between devices: 7.49 us -> 9.19 us
    pallas_call x2, Pallas kernels: 52.5 us -> 35.7 us  [conv_norm(): pl.pallas_call(conv_norm_given_kernel if given else conv_norm_kernel, out...]
    ppermute x0 -> x2, starting transfers between devices: none -> 5.54 us  [the longest x1 5.02 us: edges(): lax.ppermute(cells[:REACH], 'lon', [((i + 1) % count, i) for i in range(c...]
    all_to_all x1, starting transfers between devices: 7.49 us -> 3.65 us  [owners_data(): return lax.all_to_all(both, 'lon', split_axis=0, concat_axis=0, tiled=True)]
    pallas_call x2, Pallas kernels: 35.3 us -> 37.9 us  [conv_add(): pl.pallas_call(conv_add_kernel, out_shape=jax.ShapeDtypeStruct(shape, jnp...]
  transfers between devices with their start and end apart: 1 -> 3, of which waited for: 0 -> 0; matrix products, arithmetic and copies ran while one was open for 10% -> 10% of each run, Pallas kernels for 44% -> 36%
where the time goes in v2:
time: 145 us; the launch traced here: 144 us
  Pallas kernels  105 us (72%)
  matrix products  15.2 us (10%)
  starting transfers between devices  9.19 us (6%)
  local copies, waits for them, and re-layouts  8.33 us (6%)
  other arithmetic  6.02 us (4%)
    pallas_call x2, Pallas kernels, conv_add(): pl.pallas_call(conv_add_kernel, out_shape=jax.ShapeDtypeStruct(shape, jnp...  37.9 us
    pallas_call x2, Pallas kernels, conv_norm(): pl.pallas_call(conv_norm_given_kernel if given else conv_norm_kernel, out...  35.7 us
    pallas_call x2, Pallas kernels, mlp(): pl.pallas_call(functools.partial(mlp_kernel, piece), grid=(amount // rows...  16 us
    pallas_call x2, Pallas kernels, mlp_back(): pl.pallas_call(functools.partial(mlp_back_kernel, piece), grid=(amount //...  15.5 us
    ppermute x1, starting transfers between devices, edges(): lax.ppermute(cells[:REACH], 'lon', [((i + 1) % count, i) for i in range(c...  5.02 us
    all_to_all x1, starting transfers between devices, owners_data(): return lax.all_to_all(both, 'lon', split_axis=0, concat_axis=0, tiled=True)  3.65 us
    dot_general x2, matrix products, forward_step(): lax.dot_general(out_weight, block_out, (((0,), (1,)), ((), ())), preferre...  3.4 us
    dot_general x2, matrix products, backward_step(): lax.dot_general(lift_weight, g_lifted, (((1,), (2,)), ((), ())), preferre...  3.26 us
  transfers between devices with their start and end apart: 3, of which 0 were waited for; matrix products, arithmetic and copies ran while one was open for 10% of the time, Pallas kernels for 36%

profile of v2, /device:TPU:0, one launch (start us, length us, event | category | flops | bytes accessed | tf_op | source)
XLA Modules:
  0.0 144.3 jit_solution(17604817723857457235)
XLA Ops:
  0.0 1.3 convert_element_type.111
  1.3 1.3 convolution_convert_fusion.3.refs_0_
  2.7 0.5 collective-permute-start
  3.2 5.0 %collective-permute-start.1 = (bf16[3,128,256]{2,1,0:T(8,128)(2,1)S(1)}, bf16[3,128,256]{2,1,0:T(8,128)(2,1)S(1)}, u32[]{:S(2)}, u32[]{:S(2)}) collective-permute-start(bf16[3,128,256]{2,1,0:T(8,128)(2,1)S(1)} %get-tuple-element.27), channel_id=1, source_target_pairs={{1,0},{2,1},{3,2},{4,3},{5,4},{6,5},{7,6},{8,7},{9,8},{10,9},{11,1... | collective-permute-start | bytes 589832 | tf_op jit(solution)/shard_map/ppermute | solution.py:24
  8.2 0.2 fusion.14
  8.5 1.2 fusion.10
  9.7 3.7 %all-to-all-start = ((bf16[16,2,64,256]{3,2,1,0:T(8,128)(2,1)}), bf16[16,2,64,256]{3,2,1,0:T(8,128)(2,1)S(1)}, u32[]{:S(2)}, u32[]{:S(2)}) async-start(bf16[16,2,64,256]{3,2,1,0:T(8,128)(2,1)} %fusion.10), calls=%async_computation | async-start | bytes 2097152 | tf_op jit(solution)/shard_map/all_to_all | solution.py:414
  13.5 0.3 fusion.7
  14.0 0.3 fusion.8
  14.4 1.4 %select_reduce_fusion = (bf16[16,32,128]{2,1,0:T(8,128)(2,1)S(1)}, bf16[16,32,128]{2,1,0:T(8,128)(2,1)S(1)}) fusion(f32[16,32,4]{1,2,0:T(4,128)S(1)} %get-tuple-element.32, s32[16,32,4]{1,2,0:T(4,128)S(1)} %get-tuple-element.30, f32[16,32,4]{1,2,0:T(4,128)S(1)} %get-tuple-element.31, s32[16,32,4]{1,2,0:T(4,128)S(1)} %get-tuple-element.29), kind=kLoop, calls=%fused_computation.29 | loop fusion | flops 1441792 | bytes 294912 | tf_op jit(solution)/shard_map/reduce_sum | solution.py:376
  15.9 0.9 broadcast_in_dim.11.refs_1_.kern_ref
  16.7 14.7 %shard_map.127 = (bf16[16,128,256]{2,1,0:T(8,128)(2,1)}, bf16[16,128,256]{2,1,0:T(8,128)(2,1)}, f32[16,128,128]{2,1,0:T(8,128)}) custom-call(bf16[3,128,256]{2,1,0:T(8,128)(2,1)} %copy-done.7, bf16[3,128,256]{2,1,0:T(8,128)(2,1)} %copy-done.8, bf16[16,128,256]{2,1,0:T(8,128)(2,1)} %copy-done.2, f32[2,49,8,128]{3,2,1,0:T(8,128)} %broadcast_in_dim.11.refs_1_.kern_ref, ...), custom_call_target="tpu_custom_call" | custom-call | flops 51380224 | bytes 6291456 | tf_op jit(solution)/shard_map/pallas_call | solution.py:198
  31.4 8.0 %shard_map.128 = (bf16[2048,256]{1,0:T(8,128)(2,1)}, bf16[2048,1024]{1,0:T(8,128)(2,1)}) custom-call(bf16[2048,256]{1,0:T(8,128)(2,1)} %bitcast.158, bf16[2048,256]{1,0:T(8,128)(2,1)} %bitcast.130, bf16[256,1024]{1,0:T(8,128)(2,1)} %up_ref.7, bf16[1024,256]{1,0:T(8,128)(2,1)} %down_ref.7), custom_call_target="tpu_custom_call" | custom-call | flops 2147483648 | bytes 7340032 | tf_op jit(solution)/shard_map/pallas_call | solution.py:255
  39.4 1.7 %fusion.49 = f32[2048,95]{0,1:T(8,128)S(1)} fusion(bf16[2048,256]{1,0:T(8,128)(2,1)} %get-tuple-element.16, bf16[256,95]{0,1:T(8,128)(2,1)S(1)} %copy-done), kind=kOutput, calls=%fused_computation.89 | convolution fusion | flops 99614720 | bytes 1875456 | tf_op jit(solution)/shard_map/dot_general | solution.py:346
  41.1 0.1 copy.138
  41.3 0.9 fusion.25
  42.2 1.4 copy.124
  43.6 1.4 convolution_convert_fusion.2.mid_ref
  44.9 21.0 %shard_map.129 = (bf16[16,128,256]{2,1,0:T(8,128)(2,1)}, bf16[16,128,256]{2,1,0:T(8,128)(2,1)}, f32[16,128,128]{2,1,0:T(8,128)}) custom-call(bf16[16,128,256]{2,1,0:T(8,128)(2,1)} %convolution_convert_fusion.2.mid_ref, f32[2,49,8,128]{3,2,1,0:T(8,128)} %broadcast_in_dim.11.refs_1_.kern_ref, f32[1,256]{1,0:T(1,128)} %bitcast.151), custom_call_target="tpu_custom_call" | custom-call | flops 51380224 | bytes 6291456 | tf_op jit(solution)/shard_map/pallas_call | solution.py:198
  66.0 8.0 %shard_map.130 = (bf16[2048,256]{1,0:T(8,128)(2,1)}, bf16[2048,1024]{1,0:T(8,128)(2,1)}) custom-call(bf16[2048,256]{1,0:T(8,128)(2,1)} %bitcast.159, bf16[2048,256]{1,0:T(8,128)(2,1)} %bitcast.135, bf16[256,1024]{1,0:T(8,128)(2,1)} %up_ref.7, bf16[1024,256]{1,0:T(8,128)(2,1)} %down_ref.7), custom_call_target="tpu_custom_call" | custom-call | flops 2147483648 | bytes 7340032 | tf_op jit(solution)/shard_map/pallas_call | solution.py:255
  74.0 1.7 %fusion.50 = f32[2048,95]{0,1:T(8,128)S(1)} fusion(bf16[2048,256]{1,0:T(8,128)(2,1)} %get-tuple-element.18, bf16[256,95]{0,1:T(8,128)(2,1)S(1)} %copy-done), kind=kOutput, calls=%fused_computation.90 | convolution fusion | flops 99614720 | bytes 1875456 | tf_op jit(solution)/shard_map/dot_general | solution.py:346
  75.7 0.1 copy.139
  75.8 1.0 fusion.13
  76.8 1.4 copy.115
  78.2 0.3 fusion.18
  78.4 0.2 copy.118
  78.6 0.3 fusion.16
  78.9 0.2 copy.127
  79.0 0.1 fusion.46
  79.1 0.7 fusion
  79.9 0.1 copy.119
  80.0 0.4 convolution_bitcast_fusion.1
  80.4 1.4 convolution_convert_fusion.1.add_ref
  81.8 0.1 copy.163
  81.9 7.8 %shard_map.131 = bf16[2048,256]{1,0:T(8,128)(2,1)} custom-call(bf16[2048,256]{1,0:T(8,128)(2,1)} %bitcast.127, bf16[2048,1024]{1,0:T(8,128)(2,1)} %get-tuple-element.19.slope_ref, bf16[2048,256]{1,0:T(8,128)(2,1)} %bitcast.141, f32[2048,128]{1,0:T(8,128)} %bitcast.142, f32[1,256]{1,0:T(1,128)} %bitcast.152, bf16[256,1024]{1,0:T(8,128)(2,1)} %up_ref.7, ...), custom_call_target="tpu_custom_call" | custom-call | flops 2147483648 | bytes 8388608 | tf_op jit(solution)/shard_map/pallas_call | solution.py:309
  89.6 19.1 %shard_map.132 = bf16[16,128,256]{2,1,0:T(8,128)(2,1)} custom-call(bf16[16,128,256]{2,1,0:T(8,128)(2,1)} %bitcast.132, f32[2,49,8,128]{3,2,1,0:T(8,128)} %broadcast_in_dim.11.refs_1_.kern_ref, bf16[16,128,256]{2,1,0:T(8,128)(2,1)} %convolution_convert_fusion.1.add_ref), custom_call_target="tpu_custom_call" | custom-call | flops 51380224 | bytes 6291456 | tf_op jit(solution)/shard_map/pallas_call | solution.py:219
  108.7 0.4 copy.123
  109.0 0.7 fusion.1
  109.8 0.1 copy.128
  109.9 0.3 convolution_bitcast_fusion
  110.3 0.1 copy.162
  110.4 1.3 copy.131
  111.7 1.6 %fusion.5 = f32[95,16,128]{2,0,1:T(8,128)S(1)} fusion(f32[95,16,128]{2,0,1:T(8,128)} %copy.131, f32[95,16,128]{2,0,1:T(8,128)S(1)} %copy.123, bf16[16,128,256]{2,1,0:T(8,128)(2,1)S(1)} %copy-done.3, bf16[95,256]{1,0:T(8,128)(2,1)S(1)} %copy-done.6), kind=kOutput, calls=%fused_computation.17 | convolution fusion | flops 100003840 | bytes 3431936 | tf_op jit(solution)/shard_map/dot_general | solution.py:368
  113.3 1.4 %convolution_convert_fusion.add_ref = bf16[16,128,256]{2,1,0:T(8,128)(2,1)} fusion(f32[95,16,128]{2,0,1:T(8,128)S(1)} %fusion.5, bf16[256,95]{0,1:T(8,128)(2,1)S(1)} %copy-done), kind=kOutput, calls=%fused_computation.8 | convolution fusion | flops 100333568 | bytes 1875456 | tf_op jit(solution)/shard_map/dot_general | solution.py:358
  114.7 7.7 %shard_map.133 = bf16[2048,256]{1,0:T(8,128)(2,1)} custom-call(bf16[2048,256]{1,0:T(8,128)(2,1)} %bitcast.126, bf16[2048,1024]{1,0:T(8,128)(2,1)} %get-tuple-element.22.slope_ref, bf16[2048,256]{1,0:T(8,128)(2,1)} %bitcast.139, f32[2048,128]{1,0:T(8,128)} %bitcast.140, f32[1,256]{1,0:T(1,128)} %bitcast.153, bf16[256,1024]{1,0:T(8,128)(2,1)} %up_ref.7, ...), custom_call_target="tpu_custom_call" | custom-call | flops 2147483648 | bytes 8388608 | tf_op jit(solution)/shard_map/pallas_call | solution.py:309
  122.4 18.8 %shard_map.134 = bf16[16,128,256]{2,1,0:T(8,128)(2,1)} custom-call(bf16[16,128,256]{2,1,0:T(8,128)(2,1)} %bitcast.131, f32[2,49,8,128]{3,2,1,0:T(8,128)} %broadcast_in_dim.11.refs_1_.kern_ref, bf16[16,128,256]{2,1,0:T(8,128)(2,1)} %convolution_convert_fusion.add_ref), custom_call_target="tpu_custom_call" | custom-call | flops 51380224 | bytes 6291456 | tf_op jit(solution)/shard_map/pallas_call | solution.py:219
  141.3 1.7 %fusion.6 = f32[95,16,128]{2,0,1:T(8,128)S(1)} fusion(f32[95,16,128]{2,0,1:T(8,128)S(1)} %fusion.5, bf16[16,128,256]{2,1,0:T(8,128)(2,1)} %shard_map.134, bf16[95,256]{1,0:T(8,128)(2,1)S(1)} %copy-done.6), kind=kOutput, calls=%fused_computation.18 | convolution fusion | flops 99809280 | bytes 2653696 | tf_op jit(solution)/shard_map/dot_general | solution.py:368
  143.0 1.3 copy.132
  (45 shorter events, 0.5 us)
Async XLA Ops:
  0.0 39.4 %copy-start = (bf16[256,95]{0,1:T(8,128)(2,1)S(1)}, bf16[256,95]{0,1:T(8,128)(2,1)}, u32[]{:S(2)}) copy-start(bf16[256,95]{0,1:T(8,128)(2,1)} %param.19) | copy-start | bytes 145924
  0.0 8.2 %copy-start.4 = (f32[2,1,16,64,95]{4,3,2,1,0:T(8,128)S(1)}, f32[2,1,16,64,95]{4,3,2,1,0:T(8,128)}, u32[]{:S(2)}) copy-start(f32[2,1,16,64,95]{4,3,2,1,0:T(8,128)} %param.24) | copy-start | bytes 2334724
  0.0 8.2 %copy-start.5 = (f32[2,1,16,64,95]{4,3,2,1,0:T(8,128)S(1)}, f32[2,1,16,64,95]{4,3,2,1,0:T(8,128)}, u32[]{:S(2)}) copy-start(f32[2,1,16,64,95]{4,3,2,1,0:T(8,128)} %param.25) | copy-start | bytes 2334724
  2.6 7.1 %copy-start.2 = (bf16[16,128,256]{2,1,0:T(8,128)(2,1)}, bf16[16,128,256]{2,1,0:T(8,128)(2,1)S(1)}, u32[]{:S(2)}) copy-start(bf16[16,128,256]{2,1,0:T(8,128)(2,1)S(1)} %convolution_convert_fusion.3.refs_0_) | copy-start | bytes 3145732
  2.7 13.1 %collective-permute-start = (bf16[3,128,256]{2,1,0:T(8,128)(2,1)S(1)}, bf16[3,128,256]{2,1,0:T(8,128)(2,1)S(1)}, u32[]{:S(2)}, u32[]{:S(2)}) collective-permute-start(bf16[3,128,256]{2,1,0:T(8,128)(2,1)S(1)} %get-tuple-element.28), channel_id=1, source_target_pairs={{0,1},{1,2},{2,3},{3,4},{4,5},{5,6},{6,7},{7,8},{8,9},{9,10},{10,1... | collective-permute-start | bytes 589832 | tf_op jit(solution)/shard_map/ppermute | solution.py:23
  3.2 12.7 %collective-permute-start.1 = (bf16[3,128,256]{2,1,0:T(8,128)(2,1)S(1)}, bf16[3,128,256]{2,1,0:T(8,128)(2,1)S(1)}, u32[]{:S(2)}, u32[]{:S(2)}) collective-permute-start(bf16[3,128,256]{2,1,0:T(8,128)(2,1)S(1)} %get-tuple-element.27), channel_id=1, source_target_pairs={{1,0},{2,1},{3,2},{4,3},{5,4},{6,5},{7,6},{8,7},{9,8},{10,9},{11,1... | collective-permute-start | bytes 589832 | tf_op jit(solution)/shard_map/ppermute | solution.py:24
  8.4 5.0 %copy-start.11 = (f32[49,256]{1,0:T(8,128)S(1)}, f32[49,256]{1,0:T(8,128)}, u32[]{:S(2)}) copy-start(f32[49,256]{1,0:T(8,128)} %param.15) | copy-start | bytes 150532
  8.5 5.0 %copy-start.9 = (s32[2,16,32,4]{2,3,1,0:T(4,128)S(1)}, s32[2,16,32,4]{2,3,1,0:T(4,128)}, u32[]{:S(2)}) copy-start(s32[2,16,32,4]{2,3,1,0:T(4,128)} %param.20) | copy-start | bytes 49156
  8.5 5.0 %copy-start.10 = (f32[2,16,32,4]{2,3,1,0:T(4,128)S(1)}, f32[2,16,32,4]{2,3,1,0:T(4,128)}, u32[]{:S(2)}) copy-start(f32[2,16,32,4]{2,3,1,0:T(4,128)} %param.21) | copy-start | bytes 49156
  8.5 5.0 %copy-start.12 = (s32[2,512,1]{1,2,0:T(1,128)S(1)}, s32[2,512,1]{1,2,0:T(1,128)}, u32[]{:S(2)}) copy-start(s32[2,512,1]{1,2,0:T(1,128)} %param.23) | copy-start | bytes 12292
  8.5 5.3 %copy-start.13 = (s32[2,16]{1,0:T(2,128)S(1)}, s32[2,16]{1,0:T(2,128)}, u32[]{:S(2)}) copy-start(s32[2,16]{1,0:T(2,128)} %param.22) | copy-start | bytes 388
  9.7 69.3 %all-to-all-start = ((bf16[16,2,64,256]{3,2,1,0:T(8,128)(2,1)}), bf16[16,2,64,256]{3,2,1,0:T(8,128)(2,1)S(1)}, u32[]{:S(2)}, u32[]{:S(2)}) async-start(bf16[16,2,64,256]{3,2,1,0:T(8,128)(2,1)} %fusion.10), calls=%async_computation | async-start | bytes 2097152 | tf_op jit(solution)/shard_map/all_to_all | solution.py:414
  15.8 0.9 copy-start.7
  15.8 0.9 copy-start.8
  39.4 1.9 %copy-start.1 = (f32[95,16,128]{2,1,0:T(8,128)S(1)}, f32[95,16,128]{2,1,0:T(8,128)}, u32[]{:S(2)}) copy-start(f32[95,16,128]{2,1,0:T(8,128)} %param.13) | copy-start | bytes 2334724
  41.1 2.4 %copy-start.6 = (bf16[95,256]{1,0:T(8,128)(2,1)S(1)}, bf16[95,256]{1,0:T(8,128)(2,1)}, u32[]{:S(2)}) copy-start(bf16[95,256]{1,0:T(8,128)(2,1)} %param.14) | copy-start | bytes 145924
  110.3 1.4 copy-start.3

commit v3 on v2

--- a/solution.py
+++ b/solution.py
@@ -99,7 +99,7 @@
 def conv_all(mid_ref, kern_ref, pad_ref, mix_ref, west_ref, east_ref, sems, flip, finish):
     lon_rows, lat_cols, _ = mid_ref.shape
     copies = exchange(mid_ref, west_ref, east_ref, *sems) if sems else []
-    early = lat_cols // 64 if sems else 0
+    early = 3 * lat_cols // 64 if sems else 0
 
     def middle_row(row, carry):
         put_row(pad_ref, row + REACH, mid_ref, row)

time: 145 us -> 140 us (0.966)
  Pallas kernels: 105 us -> 99.6 us
    pallas_call x2, Pallas kernels: 37.9 us -> 32.8 us  [conv_add(): pl.pallas_call(conv_add_kernel, out_shape=jax.ShapeDtypeStruct(shape, jnp...]
  transfers between devices with their start and end apart: 3 -> 3, of which waited for: 0 -> 0; matrix products, arithmetic and copies ran while one was open for 10% -> 11% of each run, Pallas kernels for 36% -> 37%
where the time goes in v3:
time: 140 us; the launch traced here: 139 us
  Pallas kernels  99.6 us (71%)
  matrix products  15.2 us (11%)
  starting transfers between devices  9.19 us (7%)
  local copies, waits for them, and re-layouts  8.33 us (6%)
  other arithmetic  6.02 us (4%)
    pallas_call x2, Pallas kernels, conv_norm(): pl.pallas_call(conv_norm_given_kernel if given else conv_norm_kernel, out...  35.3 us
    pallas_call x2, Pallas kernels, conv_add(): pl.pallas_call(conv_add_kernel, out_shape=jax.ShapeDtypeStruct(shape, jnp...  32.8 us
    pallas_call x2, Pallas kernels, mlp(): pl.pallas_call(functools.partial(mlp_kernel, piece), grid=(amount // rows...  16 us
    pallas_call x2, Pallas kernels, mlp_back(): pl.pallas_call(functools.partial(mlp_back_kernel, piece), grid=(amount //...  15.5 us
    ppermute x1, starting transfers between devices, edges(): lax.ppermute(cells[:REACH], 'lon', [((i + 1) % count, i) for i in range(c...  5.02 us
    all_to_all x1, starting transfers between devices, owners_data(): return lax.all_to_all(both, 'lon', split_axis=0, concat_axis=0, tiled=True)  3.65 us
    dot_general x2, matrix products, forward_step(): lax.dot_general(out_weight, block_out, (((0,), (1,)), ((), ())), preferre...  3.4 us
    dot_general x2, matrix products, backward_step(): lax.dot_general(lift_weight, g_lifted, (((1,), (2,)), ((), ())), preferre...  3.25 us
  transfers between devices with their start and end apart: 3, of which 0 were waited for; matrix products, arithmetic and copies ran while one was open for 11% of the time, Pallas kernels for 37%

profile of v3, /device:TPU:0, one launch (start us, length us, event | category | flops | bytes accessed | tf_op | source)
XLA Modules:
  0.0 138.8 jit_solution(10914924900956799259)
XLA Ops:
  0.0 1.3 convert_element_type.111
  1.3 1.3 convolution_convert_fusion.3.refs_0_
  2.7 0.5 collective-permute-start
  3.2 5.0 %collective-permute-start.1 = (bf16[3,128,256]{2,1,0:T(8,128)(2,1)S(1)}, bf16[3,128,256]{2,1,0:T(8,128)(2,1)S(1)}, u32[]{:S(2)}, u32[]{:S(2)}) collective-permute-start(bf16[3,128,256]{2,1,0:T(8,128)(2,1)S(1)} %get-tuple-element.27), channel_id=1, source_target_pairs={{1,0},{2,1},{3,2},{4,3},{5,4},{6,5},{7,6},{8,7},{9,8},{10,9},{11,1... | collective-permute-start | bytes 589832 | tf_op jit(solution)/shard_map/ppermute | solution.py:24
  8.2 0.2 fusion.14
  8.5 1.2 fusion.10
  9.7 3.7 %all-to-all-start = ((bf16[16,2,64,256]{3,2,1,0:T(8,128)(2,1)}), bf16[16,2,64,256]{3,2,1,0:T(8,128)(2,1)S(1)}, u32[]{:S(2)}, u32[]{:S(2)}) async-start(bf16[16,2,64,256]{3,2,1,0:T(8,128)(2,1)} %fusion.10), calls=%async_computation | async-start | bytes 2097152 | tf_op jit(solution)/shard_map/all_to_all | solution.py:414
  13.5 0.3 fusion.7
  14.0 0.3 fusion.8
  14.4 1.4 %select_reduce_fusion = (bf16[16,32,128]{2,1,0:T(8,128)(2,1)S(1)}, bf16[16,32,128]{2,1,0:T(8,128)(2,1)S(1)}) fusion(f32[16,32,4]{1,2,0:T(4,128)S(1)} %get-tuple-element.32, s32[16,32,4]{1,2,0:T(4,128)S(1)} %get-tuple-element.30, f32[16,32,4]{1,2,0:T(4,128)S(1)} %get-tuple-element.31, s32[16,32,4]{1,2,0:T(4,128)S(1)} %get-tuple-element.29), kind=kLoop, calls=%fused_computation.29 | loop fusion | flops 1441792 | bytes 294912 | tf_op jit(solution)/shard_map/reduce_sum | solution.py:376
  15.9 0.9 broadcast_in_dim.11.refs_1_.kern_ref
  16.7 14.7 %shard_map.127 = (bf16[16,128,256]{2,1,0:T(8,128)(2,1)}, bf16[16,128,256]{2,1,0:T(8,128)(2,1)}, f32[16,128,128]{2,1,0:T(8,128)}) custom-call(bf16[3,128,256]{2,1,0:T(8,128)(2,1)} %copy-done.7, bf16[3,128,256]{2,1,0:T(8,128)(2,1)} %copy-done.8, bf16[16,128,256]{2,1,0:T(8,128)(2,1)} %copy-done.2, f32[2,49,8,128]{3,2,1,0:T(8,128)} %broadcast_in_dim.11.refs_1_.kern_ref, ...), custom_call_target="tpu_custom_call" | custom-call | flops 51380224 | bytes 6291456 | tf_op jit(solution)/shard_map/pallas_call | solution.py:198
  31.4 8.0 %shard_map.128 = (bf16[2048,256]{1,0:T(8,128)(2,1)}, bf16[2048,1024]{1,0:T(8,128)(2,1)}) custom-call(bf16[2048,256]{1,0:T(8,128)(2,1)} %bitcast.158, bf16[2048,256]{1,0:T(8,128)(2,1)} %bitcast.130, bf16[256,1024]{1,0:T(8,128)(2,1)} %up_ref.7, bf16[1024,256]{1,0:T(8,128)(2,1)} %down_ref.7), custom_call_target="tpu_custom_call" | custom-call | flops 2147483648 | bytes 7340032 | tf_op jit(solution)/shard_map/pallas_call | solution.py:255
  39.4 1.7 %fusion.49 = f32[2048,95]{0,1:T(8,128)S(1)} fusion(bf16[2048,256]{1,0:T(8,128)(2,1)} %get-tuple-element.16, bf16[256,95]{0,1:T(8,128)(2,1)S(1)} %copy-done), kind=kOutput, calls=%fused_computation.89 | convolution fusion | flops 99614720 | bytes 1875456 | tf_op jit(solution)/shard_map/dot_general | solution.py:346
  41.1 0.1 copy.138
  41.3 0.9 fusion.25
  42.2 1.4 %copy.124 = bf16[95,16,128]{0,2,1:T(8,128)(2,1)S(1)} copy(bf16[95,16,128]{2,1,0:T(8,128)(2,1)} %fusion.25) | data formatting | bytes 778240 | tf_op jit(solution)/shard_map/convert_element_type | solution.py:337
  43.6 1.4 convolution_convert_fusion.2.mid_ref
  44.9 20.7 %shard_map.129 = (bf16[16,128,256]{2,1,0:T(8,128)(2,1)}, bf16[16,128,256]{2,1,0:T(8,128)(2,1)}, f32[16,128,128]{2,1,0:T(8,128)}) custom-call(bf16[16,128,256]{2,1,0:T(8,128)(2,1)} %convolution_convert_fusion.2.mid_ref, f32[2,49,8,128]{3,2,1,0:T(8,128)} %broadcast_in_dim.11.refs_1_.kern_ref, f32[1,256]{1,0:T(1,128)} %bitcast.151), custom_call_target="tpu_custom_call" | custom-call | flops 51380224 | bytes 6291456 | tf_op jit(solution)/shard_map/pallas_call | solution.py:198
  65.6 8.0 %shard_map.130 = (bf16[2048,256]{1,0:T(8,128)(2,1)}, bf16[2048,1024]{1,0:T(8,128)(2,1)}) custom-call(bf16[2048,256]{1,0:T(8,128)(2,1)} %bitcast.159, bf16[2048,256]{1,0:T(8,128)(2,1)} %bitcast.135, bf16[256,1024]{1,0:T(8,128)(2,1)} %up_ref.7, bf16[1024,256]{1,0:T(8,128)(2,1)} %down_ref.7), custom_call_target="tpu_custom_call" | custom-call | flops 2147483648 | bytes 7340032 | tf_op jit(solution)/shard_map/pallas_call | solution.py:255
  73.6 1.7 %fusion.50 = f32[2048,95]{0,1:T(8,128)S(1)} fusion(bf16[2048,256]{1,0:T(8,128)(2,1)} %get-tuple-element.18, bf16[256,95]{0,1:T(8,128)(2,1)S(1)} %copy-done), kind=kOutput, calls=%fused_computation.90 | convolution fusion | flops 99614720 | bytes 1875456 | tf_op jit(solution)/shard_map/dot_general | solution.py:346
  75.3 0.1 copy.139
  75.5 1.0 fusion.13
  76.4 1.4 %copy.115 = bf16[95,16,128]{0,2,1:T(8,128)(2,1)S(1)} copy(bf16[95,16,128]{2,1,0:T(8,128)(2,1)} %fusion.13) | data formatting | bytes 778240 | tf_op jit(solution)/shard_map/convert_element_type | solution.py:470
  77.8 0.3 fusion.18
  78.1 0.2 copy.118
  78.2 0.3 fusion.16
  78.5 0.2 copy.127
  78.6 0.1 fusion.46
  78.8 0.7 fusion
  79.5 0.1 copy.119
  79.6 0.4 convolution_bitcast_fusion.1
  80.0 1.4 convolution_convert_fusion.1.add_ref
  81.4 0.1 copy.163
  81.5 7.8 %shard_map.131 = bf16[2048,256]{1,0:T(8,128)(2,1)} custom-call(bf16[2048,256]{1,0:T(8,128)(2,1)} %bitcast.127, bf16[2048,1024]{1,0:T(8,128)(2,1)} %get-tuple-element.19.slope_ref, bf16[2048,256]{1,0:T(8,128)(2,1)} %bitcast.141, f32[2048,128]{1,0:T(8,128)} %bitcast.142, f32[1,256]{1,0:T(1,128)} %bitcast.152, bf16[256,1024]{1,0:T(8,128)(2,1)} %up_ref.7, ...), custom_call_target="tpu_custom_call" | custom-call | flops 2147483648 | bytes 8388608 | tf_op jit(solution)/shard_map/pallas_call | solution.py:309
  89.2 16.5 %shard_map.132 = bf16[16,128,256]{2,1,0:T(8,128)(2,1)} custom-call(bf16[16,128,256]{2,1,0:T(8,128)(2,1)} %bitcast.132, f32[2,49,8,128]{3,2,1,0:T(8,128)} %broadcast_in_dim.11.refs_1_.kern_ref, bf16[16,128,256]{2,1,0:T(8,128)(2,1)} %convolution_convert_fusion.1.add_ref), custom_call_target="tpu_custom_call" | custom-call | flops 51380224 | bytes 6291456 | tf_op jit(solution)/shard_map/pallas_call | solution.py:219
  105.7 0.4 copy.123
  106.1 0.7 fusion.1
  106.9 0.1 copy.128
  107.0 0.3 convolution_bitcast_fusion
  107.4 0.1 copy.162
  107.5 1.3 copy.131
  108.7 1.6 %fusion.5 = f32[95,16,128]{2,0,1:T(8,128)S(1)} fusion(f32[95,16,128]{2,0,1:T(8,128)} %copy.131, f32[95,16,128]{2,0,1:T(8,128)S(1)} %copy.123, bf16[16,128,256]{2,1,0:T(8,128)(2,1)S(1)} %copy-done.3, bf16[95,256]{1,0:T(8,128)(2,1)S(1)} %copy-done.6), kind=kOutput, calls=%fused_computation.17 | convolution fusion | flops 100003840 | bytes 3431936 | tf_op jit(solution)/shard_map/dot_general | solution.py:368
  110.3 1.4 %convolution_convert_fusion.add_ref = bf16[16,128,256]{2,1,0:T(8,128)(2,1)} fusion(f32[95,16,128]{2,0,1:T(8,128)S(1)} %fusion.5, bf16[256,95]{0,1:T(8,128)(2,1)S(1)} %copy-done), kind=kOutput, calls=%fused_computation.8 | convolution fusion | flops 100333568 | bytes 1875456 | tf_op jit(solution)/shard_map/dot_general | solution.py:358
  111.8 7.7 %shard_map.133 = bf16[2048,256]{1,0:T(8,128)(2,1)} custom-call(bf16[2048,256]{1,0:T(8,128)(2,1)} %bitcast.126, bf16[2048,1024]{1,0:T(8,128)(2,1)} %get-tuple-element.22.slope_ref, bf16[2048,256]{1,0:T(8,128)(2,1)} %bitcast.139, f32[2048,128]{1,0:T(8,128)} %bitcast.140, f32[1,256]{1,0:T(1,128)} %bitcast.153, bf16[256,1024]{1,0:T(8,128)(2,1)} %up_ref.7, ...), custom_call_target="tpu_custom_call" | custom-call | flops 2147483648 | bytes 8388608 | tf_op jit(solution)/shard_map/pallas_call | solution.py:309
  119.5 16.3 %shard_map.134 = bf16[16,128,256]{2,1,0:T(8,128)(2,1)} custom-call(bf16[16,128,256]{2,1,0:T(8,128)(2,1)} %bitcast.131, f32[2,49,8,128]{3,2,1,0:T(8,128)} %broadcast_in_dim.11.refs_1_.kern_ref, bf16[16,128,256]{2,1,0:T(8,128)(2,1)} %convolution_convert_fusion.add_ref), custom_call_target="tpu_custom_call" | custom-call | flops 51380224 | bytes 6291456 | tf_op jit(solution)/shard_map/pallas_call | solution.py:219
  135.8 1.7 %fusion.6 = f32[95,16,128]{2,0,1:T(8,128)S(1)} fusion(f32[95,16,128]{2,0,1:T(8,128)S(1)} %fusion.5, bf16[16,128,256]{2,1,0:T(8,128)(2,1)} %shard_map.134, bf16[95,256]{1,0:T(8,128)(2,1)S(1)} %copy-done.6), kind=kOutput, calls=%fused_computation.18 | convolution fusion | flops 99809280 | bytes 2653696 | tf_op jit(solution)/shard_map/dot_general | solution.py:368
  137.5 1.3 copy.132
  (45 shorter events, 0.5 us)
Async XLA Ops:
  0.0 39.4 %copy-start = (bf16[256,95]{0,1:T(8,128)(2,1)S(1)}, bf16[256,95]{0,1:T(8,128)(2,1)}, u32[]{:S(2)}) copy-start(bf16[256,95]{0,1:T(8,128)(2,1)} %param.19) | copy-start | bytes 145924
  0.0 8.2 %copy-start.4 = (f32[2,1,16,64,95]{4,3,2,1,0:T(8,128)S(1)}, f32[2,1,16,64,95]{4,3,2,1,0:T(8,128)}, u32[]{:S(2)}) copy-start(f32[2,1,16,64,95]{4,3,2,1,0:T(8,128)} %param.24) | copy-start | bytes 2334724
  0.0 8.2 %copy-start.5 = (f32[2,1,16,64,95]{4,3,2,1,0:T(8,128)S(1)}, f32[2,1,16,64,95]{4,3,2,1,0:T(8,128)}, u32[]{:S(2)}) copy-start(f32[2,1,16,64,95]{4,3,2,1,0:T(8,128)} %param.25) | copy-start | bytes 2334724
  2.6 7.1 %copy-start.2 = (bf16[16,128,256]{2,1,0:T(8,128)(2,1)}, bf16[16,128,256]{2,1,0:T(8,128)(2,1)S(1)}, u32[]{:S(2)}) copy-start(bf16[16,128,256]{2,1,0:T(8,128)(2,1)S(1)} %convolution_convert_fusion.3.refs_0_) | copy-start | bytes 3145732
  2.7 13.1 %collective-permute-start = (bf16[3,128,256]{2,1,0:T(8,128)(2,1)S(1)}, bf16[3,128,256]{2,1,0:T(8,128)(2,1)S(1)}, u32[]{:S(2)}, u32[]{:S(2)}) collective-permute-start(bf16[3,128,256]{2,1,0:T(8,128)(2,1)S(1)} %get-tuple-element.28), channel_id=1, source_target_pairs={{0,1},{1,2},{2,3},{3,4},{4,5},{5,6},{6,7},{7,8},{8,9},{9,10},{10,1... | collective-permute-start | bytes 589832 | tf_op jit(solution)/shard_map/ppermute | solution.py:23
  3.2 12.7 %collective-permute-start.1 = (bf16[3,128,256]{2,1,0:T(8,128)(2,1)S(1)}, bf16[3,128,256]{2,1,0:T(8,128)(2,1)S(1)}, u32[]{:S(2)}, u32[]{:S(2)}) collective-permute-start(bf16[3,128,256]{2,1,0:T(8,128)(2,1)S(1)} %get-tuple-element.27), channel_id=1, source_target_pairs={{1,0},{2,1},{3,2},{4,3},{5,4},{6,5},{7,6},{8,7},{9,8},{10,9},{11,1... | collective-permute-start | bytes 589832 | tf_op jit(solution)/shard_map/ppermute | solution.py:24
  8.4 5.0 %copy-start.11 = (f32[49,256]{1,0:T(8,128)S(1)}, f32[49,256]{1,0:T(8,128)}, u32[]{:S(2)}) copy-start(f32[49,256]{1,0:T(8,128)} %param.15) | copy-start | bytes 150532
  8.5 5.0 %copy-start.9 = (s32[2,16,32,4]{2,3,1,0:T(4,128)S(1)}, s32[2,16,32,4]{2,3,1,0:T(4,128)}, u32[]{:S(2)}) copy-start(s32[2,16,32,4]{2,3,1,0:T(4,128)} %param.20) | copy-start | bytes 49156
  8.5 5.0 %copy-start.10 = (f32[2,16,32,4]{2,3,1,0:T(4,128)S(1)}, f32[2,16,32,4]{2,3,1,0:T(4,128)}, u32[]{:S(2)}) copy-start(f32[2,16,32,4]{2,3,1,0:T(4,128)} %param.21) | copy-start | bytes 49156
  8.5 5.0 %copy-start.12 = (s32[2,512,1]{1,2,0:T(1,128)S(1)}, s32[2,512,1]{1,2,0:T(1,128)}, u32[]{:S(2)}) copy-start(s32[2,512,1]{1,2,0:T(1,128)} %param.23) | copy-start | bytes 12292
  8.5 5.3 %copy-start.13 = (s32[2,16]{1,0:T(2,128)S(1)}, s32[2,16]{1,0:T(2,128)}, u32[]{:S(2)}) copy-start(s32[2,16]{1,0:T(2,128)} %param.22) | copy-start | bytes 388
  9.7 68.9 %all-to-all-start = ((bf16[16,2,64,256]{3,2,1,0:T(8,128)(2,1)}), bf16[16,2,64,256]{3,2,1,0:T(8,128)(2,1)S(1)}, u32[]{:S(2)}, u32[]{:S(2)}) async-start(bf16[16,2,64,256]{3,2,1,0:T(8,128)(2,1)} %fusion.10), calls=%async_computation | async-start | bytes 2097152 | tf_op jit(solution)/shard_map/all_to_all | solution.py:414
  15.8 0.9 copy-start.7
  15.8 0.9 copy-start.8
  39.4 1.9 %copy-start.1 = (f32[95,16,128]{2,1,0:T(8,128)S(1)}, f32[95,16,128]{2,1,0:T(8,128)}, u32[]{:S(2)}) copy-start(f32[95,16,128]{2,1,0:T(8,128)} %param.13) | copy-start | bytes 2334724
  41.1 2.4 %copy-start.6 = (bf16[95,256]{1,0:T(8,128)(2,1)S(1)}, bf16[95,256]{1,0:T(8,128)(2,1)}, u32[]{:S(2)}) copy-start(bf16[95,256]{1,0:T(8,128)(2,1)} %param.14) | copy-start | bytes 145924
  107.3 1.4 copy-start.3

commit v4 on v3

--- a/solution.py
+++ b/solution.py
@@ -238,9 +238,11 @@
         tanh_val = jnp.tanh(z * (root_two_pi + root_two_pi * gelu_coef * square))
         half = 0.5 + 0.5 * tanh_val
         active = (z * half).astype(jnp.bfloat16)
-        bend = z * (root_two_pi + 3.0 * root_two_pi * gelu_coef * square)
-        slope = half + half * (1.0 - tanh_val) * bend
-        slope_ref[:, start : start + piece] = slope.astype(jnp.bfloat16)
+        rest = (1.0 - half).astype(jnp.bfloat16)
+        share, arg = half.astype(jnp.bfloat16), z.astype(jnp.bfloat16)
+        steep = jnp.bfloat16(6.0 * root_two_pi * gelu_coef)
+        bend = arg * (jnp.bfloat16(2.0 * root_two_pi) + steep * (arg * arg))
+        slope_ref[:, start : start + piece] = share + share * (rest * bend)
         total = total + jnp.dot(
             active, down_ref[start : start + piece, :], preferred_element_type=jnp.float32
         )

time: 140 us -> 139 us (level)
  no operation moved by 1% of the time
where the time goes in v4:
time: 139 us; the launch traced here: 138 us
  Pallas kernels  99.1 us (71%)
  matrix products  15.2 us (11%)
  starting transfers between devices  9.19 us (7%)
  local copies, waits for them, and re-layouts  8.33 us (6%)
  other arithmetic  6.02 us (4%)
    pallas_call x2, Pallas kernels, conv_norm(): pl.pallas_call(conv_norm_given_kernel if given else conv_norm_kernel, out...  35.3 us
    pallas_call x2, Pallas kernels, conv_add(): pl.pallas_call(conv_add_kernel, out_shape=jax.ShapeDtypeStruct(shape, jnp...  32.8 us
    pallas_call x2, Pallas kernels, mlp(): pl.pallas_call(functools.partial(mlp_kernel, piece), grid=(amount // rows...  15.5 us
    pallas_call x2, Pallas kernels, mlp_back(): pl.pallas_call(functools.partial(mlp_back_kernel, piece), grid=(amount //...  15.5 us
    ppermute x1, starting transfers between devices, edges(): lax.ppermute(cells[:REACH], 'lon', [((i + 1) % count, i) for i in range(c...  5.02 us
    all_to_all x1, starting transfers between devices, owners_data(): return lax.all_to_all(both, 'lon', split_axis=0, concat_axis=0, tiled=True)  3.65 us
    dot_general x2, matrix products, forward_step(): lax.dot_general(out_weight, block_out, (((0,), (1,)), ((), ())), preferre...  3.41 us
    dot_general x2, matrix products, backward_step(): lax.dot_general(lift_weight, g_lifted, (((1,), (2,)), ((), ())), preferre...  3.25 us
  transfers between devices with their start and end apart: 3, of which 0 were waited for; matrix products, arithmetic and copies ran while one was open for 11% of the time, Pallas kernels for 37%

profile of v4, /device:TPU:0, one launch (start us, length us, event | category | flops | bytes accessed | tf_op | source)
XLA Modules:
  0.0 138.3 jit_solution(746048093873814841)
XLA Ops:
  0.0 1.3 convert_element_type.111
  1.3 1.3 convolution_convert_fusion.3.refs_0_
  2.7 0.5 collective-permute-start
  3.2 5.0 %collective-permute-start.1 = (bf16[3,128,256]{2,1,0:T(8,128)(2,1)S(1)}, bf16[3,128,256]{2,1,0:T(8,128)(2,1)S(1)}, u32[]{:S(2)}, u32[]{:S(2)}) collective-permute-start(bf16[3,128,256]{2,1,0:T(8,128)(2,1)S(1)} %get-tuple-element.27), channel_id=1, source_target_pairs={{1,0},{2,1},{3,2},{4,3},{5,4},{6,5},{7,6},{8,7},{9,8},{10,9},{11,1... | collective-permute-start | bytes 589832 | tf_op jit(solution)/shard_map/ppermute | solution.py:24
  8.2 0.2 fusion.14
  8.5 1.2 fusion.10
  9.7 3.7 %all-to-all-start = ((bf16[16,2,64,256]{3,2,1,0:T(8,128)(2,1)}), bf16[16,2,64,256]{3,2,1,0:T(8,128)(2,1)S(1)}, u32[]{:S(2)}, u32[]{:S(2)}) async-start(bf16[16,2,64,256]{3,2,1,0:T(8,128)(2,1)} %fusion.10), calls=%async_computation | async-start | bytes 2097152 | tf_op jit(solution)/shard_map/all_to_all | solution.py:416
  13.5 0.3 fusion.7
  14.0 0.3 fusion.8
  14.4 1.4 %select_reduce_fusion = (bf16[16,32,128]{2,1,0:T(8,128)(2,1)S(1)}, bf16[16,32,128]{2,1,0:T(8,128)(2,1)S(1)}) fusion(f32[16,32,4]{1,2,0:T(4,128)S(1)} %get-tuple-element.32, s32[16,32,4]{1,2,0:T(4,128)S(1)} %get-tuple-element.30, f32[16,32,4]{1,2,0:T(4,128)S(1)} %get-tuple-element.31, s32[16,32,4]{1,2,0:T(4,128)S(1)} %get-tuple-element.29), kind=kLoop, calls=%fused_computation.29 | loop fusion | flops 1441792 | bytes 294912 | tf_op jit(solution)/shard_map/reduce_sum | solution.py:378
  15.9 0.9 broadcast_in_dim.11.refs_1_.kern_ref
  16.7 14.7 %shard_map.127 = (bf16[16,128,256]{2,1,0:T(8,128)(2,1)}, bf16[16,128,256]{2,1,0:T(8,128)(2,1)}, f32[16,128,128]{2,1,0:T(8,128)}) custom-call(bf16[3,128,256]{2,1,0:T(8,128)(2,1)} %copy-done.7, bf16[3,128,256]{2,1,0:T(8,128)(2,1)} %copy-done.8, bf16[16,128,256]{2,1,0:T(8,128)(2,1)} %copy-done.2, f32[2,49,8,128]{3,2,1,0:T(8,128)} %broadcast_in_dim.11.refs_1_.kern_ref, ...), custom_call_target="tpu_custom_call" | custom-call | flops 51380224 | bytes 6291456 | tf_op jit(solution)/shard_map/pallas_call | solution.py:198
  31.4 7.8 %shard_map.128 = (bf16[2048,256]{1,0:T(8,128)(2,1)}, bf16[2048,1024]{1,0:T(8,128)(2,1)}) custom-call(bf16[2048,256]{1,0:T(8,128)(2,1)} %bitcast.158, bf16[2048,256]{1,0:T(8,128)(2,1)} %bitcast.130, bf16[256,1024]{1,0:T(8,128)(2,1)} %up_ref.7, bf16[1024,256]{1,0:T(8,128)(2,1)} %down_ref.7), custom_call_target="tpu_custom_call" | custom-call | flops 2147483648 | bytes 7340032 | tf_op jit(solution)/shard_map/pallas_call | solution.py:257
  39.2 1.7 %fusion.49 = f32[2048,95]{0,1:T(8,128)S(1)} fusion(bf16[2048,256]{1,0:T(8,128)(2,1)} %get-tuple-element.16, bf16[256,95]{0,1:T(8,128)(2,1)S(1)} %copy-done), kind=kOutput, calls=%fused_computation.89 | convolution fusion | flops 99614720 | bytes 1875456 | tf_op jit(solution)/shard_map/dot_general | solution.py:348
  40.9 0.1 copy.138
  41.1 0.9 fusion.25
  41.9 1.4 %copy.124 = bf16[95,16,128]{0,2,1:T(8,128)(2,1)S(1)} copy(bf16[95,16,128]{2,1,0:T(8,128)(2,1)} %fusion.25) | data formatting | bytes 778240 | tf_op jit(solution)/shard_map/convert_element_type | solution.py:339
  43.3 1.4 convolution_convert_fusion.2.mid_ref
  44.7 20.7 %shard_map.129 = (bf16[16,128,256]{2,1,0:T(8,128)(2,1)}, bf16[16,128,256]{2,1,0:T(8,128)(2,1)}, f32[16,128,128]{2,1,0:T(8,128)}) custom-call(bf16[16,128,256]{2,1,0:T(8,128)(2,1)} %convolution_convert_fusion.2.mid_ref, f32[2,49,8,128]{3,2,1,0:T(8,128)} %broadcast_in_dim.11.refs_1_.kern_ref, f32[1,256]{1,0:T(1,128)} %bitcast.151), custom_call_target="tpu_custom_call" | custom-call | flops 51380224 | bytes 6291456 | tf_op jit(solution)/shard_map/pallas_call | solution.py:198
  65.4 7.8 %shard_map.130 = (bf16[2048,256]{1,0:T(8,128)(2,1)}, bf16[2048,1024]{1,0:T(8,128)(2,1)}) custom-call(bf16[2048,256]{1,0:T(8,128)(2,1)} %bitcast.159, bf16[2048,256]{1,0:T(8,128)(2,1)} %bitcast.135, bf16[256,1024]{1,0:T(8,128)(2,1)} %up_ref.7, bf16[1024,256]{1,0:T(8,128)(2,1)} %down_ref.7), custom_call_target="tpu_custom_call" | custom-call | flops 2147483648 | bytes 7340032 | tf_op jit(solution)/shard_map/pallas_call | solution.py:257
  73.2 1.7 %fusion.50 = f32[2048,95]{0,1:T(8,128)S(1)} fusion(bf16[2048,256]{1,0:T(8,128)(2,1)} %get-tuple-element.18, bf16[256,95]{0,1:T(8,128)(2,1)S(1)} %copy-done), kind=kOutput, calls=%fused_computation.90 | convolution fusion | flops 99614720 | bytes 1875456 | tf_op jit(solution)/shard_map/dot_general | solution.py:348
  74.9 0.1 copy.139
  75.0 1.0 fusion.13
  76.0 1.4 %copy.115 = bf16[95,16,128]{0,2,1:T(8,128)(2,1)S(1)} copy(bf16[95,16,128]{2,1,0:T(8,128)(2,1)} %fusion.13) | data formatting | bytes 778240 | tf_op jit(solution)/shard_map/convert_element_type | solution.py:472
  77.4 0.3 fusion.18
  77.6 0.2 copy.118
  77.8 0.3 fusion.16
  78.0 0.2 copy.127
  78.2 0.1 fusion.46
  78.3 0.7 fusion
  79.0 0.1 copy.119
  79.2 0.4 convolution_bitcast_fusion.1
  79.5 1.4 %convolution_convert_fusion.1.add_ref = bf16[16,128,256]{2,1,0:T(8,128)(2,1)} fusion(bf16[256,95]{0,1:T(8,128)(2,1)S(1)} %copy-done, f32[95,16,16,8]{0,3,1,2:T(8,128)S(1)} %convolution_bitcast_fusion.1), kind=kOutput, calls=%fused_computation.9 | convolution fusion | flops 100139008 | bytes 1875456 | tf_op jit(solution)/shard_map/dot_general | solution.py:360
  80.9 0.1 copy.163
  81.0 7.8 %shard_map.131 = bf16[2048,256]{1,0:T(8,128)(2,1)} custom-call(bf16[2048,256]{1,0:T(8,128)(2,1)} %bitcast.127, bf16[2048,1024]{1,0:T(8,128)(2,1)} %get-tuple-element.19.slope_ref, bf16[2048,256]{1,0:T(8,128)(2,1)} %bitcast.141, f32[2048,128]{1,0:T(8,128)} %bitcast.142, f32[1,256]{1,0:T(1,128)} %bitcast.152, bf16[256,1024]{1,0:T(8,128)(2,1)} %up_ref.7, ...), custom_call_target="tpu_custom_call" | custom-call | flops 2147483648 | bytes 8388608 | tf_op jit(solution)/shard_map/pallas_call | solution.py:311
  88.8 16.5 %shard_map.132 = bf16[16,128,256]{2,1,0:T(8,128)(2,1)} custom-call(bf16[16,128,256]{2,1,0:T(8,128)(2,1)} %bitcast.132, f32[2,49,8,128]{3,2,1,0:T(8,128)} %broadcast_in_dim.11.refs_1_.kern_ref, bf16[16,128,256]{2,1,0:T(8,128)(2,1)} %convolution_convert_fusion.1.add_ref), custom_call_target="tpu_custom_call" | custom-call | flops 51380224 | bytes 6291456 | tf_op jit(solution)/shard_map/pallas_call | solution.py:219
  105.3 0.4 copy.123
  105.6 0.7 fusion.1
  106.4 0.1 copy.128
  106.5 0.3 convolution_bitcast_fusion
  106.9 0.1 copy.162
  107.0 1.3 copy.131
  108.3 1.6 %fusion.5 = f32[95,16,128]{2,0,1:T(8,128)S(1)} fusion(f32[95,16,128]{2,0,1:T(8,128)} %copy.131, f32[95,16,128]{2,0,1:T(8,128)S(1)} %copy.123, bf16[16,128,256]{2,1,0:T(8,128)(2,1)S(1)} %copy-done.3, bf16[95,256]{1,0:T(8,128)(2,1)S(1)} %copy-done.6), kind=kOutput, calls=%fused_computation.17 | convolution fusion | flops 100003840 | bytes 3431936 | tf_op jit(solution)/shard_map/dot_general | solution.py:370
  109.8 1.4 %convolution_convert_fusion.add_ref = bf16[16,128,256]{2,1,0:T(8,128)(2,1)} fusion(f32[95,16,128]{2,0,1:T(8,128)S(1)} %fusion.5, bf16[256,95]{0,1:T(8,128)(2,1)S(1)} %copy-done), kind=kOutput, calls=%fused_computation.8 | convolution fusion | flops 100333568 | bytes 1875456 | tf_op jit(solution)/shard_map/dot_general | solution.py:360
  111.3 7.7 %shard_map.133 = bf16[2048,256]{1,0:T(8,128)(2,1)} custom-call(bf16[2048,256]{1,0:T(8,128)(2,1)} %bitcast.126, bf16[2048,1024]{1,0:T(8,128)(2,1)} %get-tuple-element.22.slope_ref, bf16[2048,256]{1,0:T(8,128)(2,1)} %bitcast.139, f32[2048,128]{1,0:T(8,128)} %bitcast.140, f32[1,256]{1,0:T(1,128)} %bitcast.153, bf16[256,1024]{1,0:T(8,128)(2,1)} %up_ref.7, ...), custom_call_target="tpu_custom_call" | custom-call | flops 2147483648 | bytes 8388608 | tf_op jit(solution)/shard_map/pallas_call | solution.py:311
  119.0 16.3 %shard_map.134 = bf16[16,128,256]{2,1,0:T(8,128)(2,1)} custom-call(bf16[16,128,256]{2,1,0:T(8,128)(2,1)} %bitcast.131, f32[2,49,8,128]{3,2,1,0:T(8,128)} %broadcast_in_dim.11.refs_1_.kern_ref, bf16[16,128,256]{2,1,0:T(8,128)(2,1)} %convolution_convert_fusion.add_ref), custom_call_target="tpu_custom_call" | custom-call | flops 51380224 | bytes 6291456 | tf_op jit(solution)/shard_map/pallas_call | solution.py:219
  135.3 1.7 %fusion.6 = f32[95,16,128]{2,0,1:T(8,128)S(1)} fusion(f32[95,16,128]{2,0,1:T(8,128)S(1)} %fusion.5, bf16[16,128,256]{2,1,0:T(8,128)(2,1)} %shard_map.134, bf16[95,256]{1,0:T(8,128)(2,1)S(1)} %copy-done.6), kind=kOutput, calls=%fused_computation.18 | convolution fusion | flops 99809280 | bytes 2653696 | tf_op jit(solution)/shard_map/dot_general | solution.py:370
  137.0 1.3 copy.132
  (45 shorter events, 0.5 us)
Async XLA Ops:
  0.0 39.2 %copy-start = (bf16[256,95]{0,1:T(8,128)(2,1)S(1)}, bf16[256,95]{0,1:T(8,128)(2,1)}, u32[]{:S(2)}) copy-start(bf16[256,95]{0,1:T(8,128)(2,1)} %param.19) | copy-start | bytes 145924
  0.0 8.2 %copy-start.4 = (f32[2,1,16,64,95]{4,3,2,1,0:T(8,128)S(1)}, f32[2,1,16,64,95]{4,3,2,1,0:T(8,128)}, u32[]{:S(2)}) copy-start(f32[2,1,16,64,95]{4,3,2,1,0:T(8,128)} %param.24) | copy-start | bytes 2334724
  0.0 8.2 %copy-start.5 = (f32[2,1,16,64,95]{4,3,2,1,0:T(8,128)S(1)}, f32[2,1,16,64,95]{4,3,2,1,0:T(8,128)}, u32[]{:S(2)}) copy-start(f32[2,1,16,64,95]{4,3,2,1,0:T(8,128)} %param.25) | copy-start | bytes 2334724
  2.6 7.1 %copy-start.2 = (bf16[16,128,256]{2,1,0:T(8,128)(2,1)}, bf16[16,128,256]{2,1,0:T(8,128)(2,1)S(1)}, u32[]{:S(2)}) copy-start(bf16[16,128,256]{2,1,0:T(8,128)(2,1)S(1)} %convolution_convert_fusion.3.refs_0_) | copy-start | bytes 3145732
  2.7 13.1 %collective-permute-start = (bf16[3,128,256]{2,1,0:T(8,128)(2,1)S(1)}, bf16[3,128,256]{2,1,0:T(8,128)(2,1)S(1)}, u32[]{:S(2)}, u32[]{:S(2)}) collective-permute-start(bf16[3,128,256]{2,1,0:T(8,128)(2,1)S(1)} %get-tuple-element.28), channel_id=1, source_target_pairs={{0,1},{1,2},{2,3},{3,4},{4,5},{5,6},{6,7},{7,8},{8,9},{9,10},{10,1... | collective-permute-start | bytes 589832 | tf_op jit(solution)/shard_map/ppermute | solution.py:23
  3.2 12.7 %collective-permute-start.1 = (bf16[3,128,256]{2,1,0:T(8,128)(2,1)S(1)}, bf16[3,128,256]{2,1,0:T(8,128)(2,1)S(1)}, u32[]{:S(2)}, u32[]{:S(2)}) collective-permute-start(bf16[3,128,256]{2,1,0:T(8,128)(2,1)S(1)} %get-tuple-element.27), channel_id=1, source_target_pairs={{1,0},{2,1},{3,2},{4,3},{5,4},{6,5},{7,6},{8,7},{9,8},{10,9},{11,1... | collective-permute-start | bytes 589832 | tf_op jit(solution)/shard_map/ppermute | solution.py:24
  8.4 5.0 %copy-start.11 = (f32[49,256]{1,0:T(8,128)S(1)}, f32[49,256]{1,0:T(8,128)}, u32[]{:S(2)}) copy-start(f32[49,256]{1,0:T(8,128)} %param.15) | copy-start | bytes 150532
  8.5 5.0 %copy-start.9 = (s32[2,16,32,4]{2,3,1,0:T(4,128)S(1)}, s32[2,16,32,4]{2,3,1,0:T(4,128)}, u32[]{:S(2)}) copy-start(s32[2,16,32,4]{2,3,1,0:T(4,128)} %param.20) | copy-start | bytes 49156
  8.5 5.0 %copy-start.10 = (f32[2,16,32,4]{2,3,1,0:T(4,128)S(1)}, f32[2,16,32,4]{2,3,1,0:T(4,128)}, u32[]{:S(2)}) copy-start(f32[2,16,32,4]{2,3,1,0:T(4,128)} %param.21) | copy-start | bytes 49156
  8.5 5.0 %copy-start.12 = (s32[2,512,1]{1,2,0:T(1,128)S(1)}, s32[2,512,1]{1,2,0:T(1,128)}, u32[]{:S(2)}) copy-start(s32[2,512,1]{1,2,0:T(1,128)} %param.23) | copy-start | bytes 12292
  8.5 5.3 %copy-start.13 = (s32[2,16]{1,0:T(2,128)S(1)}, s32[2,16]{1,0:T(2,128)}, u32[]{:S(2)}) copy-start(s32[2,16]{1,0:T(2,128)} %param.22) | copy-start | bytes 388
  9.7 68.4 %all-to-all-start = ((bf16[16,2,64,256]{3,2,1,0:T(8,128)(2,1)}), bf16[16,2,64,256]{3,2,1,0:T(8,128)(2,1)S(1)}, u32[]{:S(2)}, u32[]{:S(2)}) async-start(bf16[16,2,64,256]{3,2,1,0:T(8,128)(2,1)} %fusion.10), calls=%async_computation | async-start | bytes 2097152 | tf_op jit(solution)/shard_map/all_to_all | solution.py:416
  15.8 0.9 copy-start.7
  15.8 0.9 copy-start.8
  39.2 1.9 %copy-start.1 = (f32[95,16,128]{2,1,0:T(8,128)S(1)}, f32[95,16,128]{2,1,0:T(8,128)}, u32[]{:S(2)}) copy-start(f32[95,16,128]{2,1,0:T(8,128)} %param.13) | copy-start | bytes 2334724
  40.9 2.4 %copy-start.6 = (bf16[95,256]{1,0:T(8,128)(2,1)S(1)}, bf16[95,256]{1,0:T(8,128)(2,1)}, u32[]{:S(2)}) copy-start(bf16[95,256]{1,0:T(8,128)(2,1)} %param.14) | copy-start | bytes 145924
  106.9 1.4 copy-start.3
